TPU v7x, 32 devices: a whole 2x2x4 slice. The times are simulated.
32 devices in a mesh: seq: 4 (over y, x), fsdp: 8 (over z, core).
Axes of the slice: x: 2, y: 2, z: 4, core: 2. Of those that a mesh axis runs over, the one named last changes fastest.
Arguments:
- hidden_in: bfloat16 [8, 1024, 2048], P('fsdp', 'seq'), may hold values from -6 to 6
- segments: int32 [8, 1024], P('fsdp'), may hold values from 0 to 2, as said below
- out_grad: bfloat16 [8, 1024, 2048], P('fsdp', 'seq'), may hold values from -6 to 6
- norm1_gain: bfloat16 [2048], P(('seq', 'fsdp')), may hold values from 0.25 to 1.75
- w_query: bfloat16 [2048, 1024], P(('seq', 'fsdp')), may hold values from -0.125 to 0.125
- w_keyval: bfloat16 [2048, 512], P(('seq', 'fsdp')), may hold values from -0.125 to 0.125
- w_attn_out: bfloat16 [1024, 2048], P(('seq', 'fsdp')), may hold values from -0.75 to 0.75
- w_gate_z: bfloat16 [2048, 3072], P(('seq', 'fsdp')), may hold values from -0.125 to 0.125
- w_ssm_x: bfloat16 [2048, 3072], P(('seq', 'fsdp')), may hold values from -0.125 to 0.125
- w_ssm_bc: bfloat16 [2048, 512], P(('seq', 'fsdp')), may hold values from -0.125 to 0.125
- w_ssm_dt: bfloat16 [2048, 48], P(('seq', 'fsdp')), may hold values from -0.0625 to 0.0625
- conv_taps: bfloat16 [3584, 5], P(('seq', 'fsdp')), may hold values from -0.59765625 to 0.59765625
- a_log: float32 [48], replicated, may hold values from 0 to 1.4
- dt_bias: float32 [48], replicated, may hold values from -6 to -3
- skip_gain: float32 [48], replicated, may hold values from 0.5 to 1.5
- ssm_gain: bfloat16 [3072], P(('seq', 'fsdp')), may hold values from 0.25 to 1.75
- w_ssm_out: bfloat16 [3072, 2048], P(('seq', 'fsdp')), may hold values from -0.109375 to 0.109375
- norm2_gain: bfloat16 [2048], P(('seq', 'fsdp')), may hold values from 0.25 to 1.75
- w_ff_gate: bfloat16 [2048, 4096], P(('seq', 'fsdp')), may hold values from -0.125 to 0.125
- w_ff_up: bfloat16 [2048, 4096], P(('seq', 'fsdp')), may hold values from -0.125 to 0.125
- w_ff_down: bfloat16 [4096, 2048], P(('seq', 'fsdp')), may hold values from -0.09375 to 0.09375
Outputs:
- layer_out: bfloat16 [8, 1024, 2048], P('fsdp', 'seq')
- grad_in: bfloat16 [8, 1024, 2048], P('fsdp', 'seq')
- grad_norm1_gain: float32 [2048], P(('seq', 'fsdp'))
- grad_w_query: float32 [2048, 1024], P(('seq', 'fsdp'))
- grad_w_keyval: float32 [2048, 512], P(('seq', 'fsdp'))
- grad_w_attn_out: float32 [1024, 2048], P(('seq', 'fsdp'))
- grad_w_gate_z: float32 [2048, 3072], P(('seq', 'fsdp'))
- grad_w_ssm_x: float32 [2048, 3072], P(('seq', 'fsdp'))
- grad_w_ssm_bc: float32 [2048, 512], P(('seq', 'fsdp'))
- grad_w_ssm_dt: float32 [2048, 48], P(('seq', 'fsdp'))
- grad_conv_taps: float32 [3584, 5], P(('seq', 'fsdp'))
- grad_a_log: float32 [48], replicated
- grad_dt_bias: float32 [48], replicated
- grad_skip_gain: float32 [48], replicated
- grad_ssm_gain: float32 [3072], P(('seq', 'fsdp'))
- grad_w_ssm_out: float32 [3072, 2048], P(('seq', 'fsdp'))
- grad_norm2_gain: float32 [2048], P(('seq', 'fsdp'))
- grad_w_ff_gate: float32 [2048, 4096], P(('seq', 'fsdp'))
- grad_w_ff_up: float32 [2048, 4096], P(('seq', 'fsdp'))
- grad_w_ff_down: float32 [4096, 2048], P(('seq', 'fsdp'))
Inputs may be any that keep to these rules, and one draw needn't show every extreme that they name: `segments`: along each row the ids never fall: documents 0, 1 and 2 in this order, each of one token or more; document 1 covers all but 1 to max(1, 64) tokens at each end of the row.
All inputs are finite; a program needn't handle non-finite values.
Results may differ from a plain program's by a relative error of at most 0.018.
Values may be sent and summed in bfloat16 or wider, within the bound.
No kernel may reach another device: no remote copies, remote signals or barrier semaphores. Data moves between devices by JAX's collectives and lax.ppermute only.
A program may use at most 448 MiB of HBM per device.

v0:
```python
import functools

import jax
import jax.numpy as jnp
import numpy as np
from jax import lax
from jax.experimental import pallas as pl
from jax.experimental.layout import Layout, with_layout_constraint
from jax.experimental.pallas import tpu as pltpu
from jax.sharding import PartitionSpec as P

HEADS = 8
KV_HEADS = 2
HEAD_DIM = 128
SSM_DIM = 64
STATE = 256
BLOCK = 256
LANES = 128
KERNEL_VMEM = 56 * 1024 * 1024


epsilon = 1e-05
rope_base = 10000.0
masked_score = -1e30


def mat_product(left_op, right_op):
    return jnp.dot(left_op, right_op, preferred_element_type=jnp.float32)


def weight_grad(left_op, right_op):
    return lax.dot_general(
        left_op, right_op, (((0,), (0,)), ((), ())), preferred_element_type=jnp.float32
    )


def input_grad(grad_rows, weights):
    return lax.dot_general(
        grad_rows, weights, (((1,), (1,)), ((), ())), preferred_element_type=jnp.float32
    )


def dot_plain(left_op, right_op):
    return jnp.dot(left_op, right_op, preferred_element_type=jnp.float32)


def dot_ones(left_op, ones, terms):
    total = None
    for _ in range(terms):
        part = left_op.astype(jnp.bfloat16)
        product = dot_plain(part, ones)
        total = product if total is None else total + product
        left_op = left_op - part.astype(jnp.float32)
    return total


def ones_dot(ones, right_op, terms):
    total = None
    for _ in range(terms):
        part = right_op.astype(jnp.bfloat16)
        product = dot_plain(ones, part)
        total = product if total is None else total + product
        right_op = right_op - part.astype(jnp.float32)
    return total


def logistic(values):
    return 0.5 * jnp.tanh(0.5 * values) + 0.5


def dot_rows(left_op, right_op):
    return lax.dot_general(
        left_op, right_op, (((1,), (1,)), ((), ())), preferred_element_type=jnp.float32
    )


def dot_columns(left_op, right_op):
    return lax.dot_general(
        left_op, right_op, (((0,), (0,)), ((), ())), preferred_element_type=jnp.float32
    )


def iota_of(shape, axis):
    return lax.broadcasted_iota(jnp.int32, shape, axis)


def allowed_block(marks_ref, seg_row_ref, row_start, col_start, columns, diagonal):
    seg_col = marks_ref[pl.ds(row_start, BLOCK), 0:1]
    seg_row = seg_row_ref[0:1, pl.ds(col_start, columns)]
    same = seg_col == seg_row
    if diagonal:
        row_pos = row_start + iota_of((BLOCK, columns), 0)
        col_pos = col_start + iota_of((BLOCK, columns), 1)
        same = same & (row_pos >= col_pos)
    return same


def store_relative(order_ref, target, piece, row_start, column, values):
    rows, width = values.shape
    for part in range(rows // piece):
        place = row_start // piece + part
        start = pl.multiple_of(order_ref[place] * piece, piece)
        target[pl.ds(start, piece), column : column + width] = values[
            part * piece : (part + 1) * piece
        ]


def attention_load(pieces, order_ref, narrow_ref, cos_ref, sin_ref, q_s, k_s, v_s, q_width):
    length = narrow_ref.shape[0]
    piece = length // pieces
    for place in range(pieces):
        start = pl.multiple_of(order_ref[place] * piece, piece)
        rows = slice(place * piece, (place + 1) * piece)
        cosine = cos_ref[rows, :]
        sine = sin_ref[rows, :]
        for column in range(0, q_width + HEAD_DIM, HEAD_DIM):
            part = narrow_ref[pl.ds(start, piece), column : column + HEAD_DIM].astype(jnp.float32)
            turned = part * cosine + pltpu.roll(part, HEAD_DIM // 2, 1) * sine
            if column < q_width:
                q_s[rows, column : column + HEAD_DIM] = turned.astype(jnp.bfloat16)
            else:
                k_s[rows, :] = turned.astype(jnp.bfloat16)
        v_s[rows, :] = narrow_ref[
            pl.ds(start, piece), q_width + HEAD_DIM : q_width + 2 * HEAD_DIM
        ]


def attention_forward_kernel(
    q_width,
    pieces,
    order_ref,
    narrow_ref,
    cos_ref,
    sin_ref,
    marks_ref,
    seg_row_ref,
    out_ref,
    lse_ref,
    q_s,
    k_s,
    v_s,
):
    length = narrow_ref.shape[0]
    piece = length // pieces
    attention_load(pieces, order_ref, narrow_ref, cos_ref, sin_ref, q_s, k_s, v_s, q_width)
    for block in range(length // BLOCK):
        start = block * BLOCK
        columns = start + BLOCK
        allowed = allowed_block(marks_ref, seg_row_ref, start, 0, columns, True)
        for head in range(q_width // HEAD_DIM):
            lanes = slice(head * HEAD_DIM, (head + 1) * HEAD_DIM)
            scores = dot_rows(q_s[start : start + BLOCK, lanes], k_s[0:columns, :])
            scores = jnp.where(allowed, scores * HEAD_DIM ** (-0.5), masked_score)
            row_max = jnp.max(scores, axis=1, keepdims=True)
            exponent = jnp.exp(scores - row_max)
            total = jnp.sum(exponent, axis=1, keepdims=True)
            probs = (exponent * (1.0 / total)).astype(jnp.bfloat16)
            mixed = dot_plain(probs, v_s[0:columns, :]).astype(jnp.bfloat16)
            store_relative(order_ref, out_ref, piece, start, head * HEAD_DIM, mixed)
            lse_ref[start : start + BLOCK, head : head + 1] = row_max + jnp.log(total)


def attention_backward_kernel(
    q_width,
    pieces,
    order_ref,
    narrow_ref,
    grad_ref,
    cos_ref,
    sin_ref,
    marks_ref,
    seg_row_ref,
    lse_ref,
    out_ref,
    q_s,
    k_s,
    v_s,
    g_s,
    dk_s,
    dv_s,
):
    length = narrow_ref.shape[0]
    piece = length // pieces
    scale = HEAD_DIM ** (-0.5)
    attention_load(pieces, order_ref, narrow_ref, cos_ref, sin_ref, q_s, k_s, v_s, q_width)
    for place in range(pieces):
        rows = slice(place * piece, (place + 1) * piece)
        start = pl.multiple_of(order_ref[place] * piece, piece)
        g_s[rows, :] = grad_ref[pl.ds(start, piece), 0:q_width]
    dk_s[...] = jnp.zeros_like(dk_s)
    dv_s[...] = jnp.zeros_like(dv_s)
    for block in range(length // BLOCK):
        start = block * BLOCK
        columns = start + BLOCK
        rows = slice(start, columns)
        cosine = cos_ref[rows, :]
        sine = sin_ref[rows, :]
        allowed = allowed_block(marks_ref, seg_row_ref, start, 0, columns, True)
        for head in range(q_width // HEAD_DIM):
            lanes = slice(head * HEAD_DIM, (head + 1) * HEAD_DIM)
            q_blk = q_s[rows, lanes]
            g_blk = g_s[rows, lanes]
            scores = dot_rows(q_blk, k_s[0:columns, :])
            scores = jnp.where(allowed, scores * scale, masked_score)
            probs = jnp.exp(scores - lse_ref[rows, head : head + 1])
            grad_probs = dot_rows(g_blk, v_s[0:columns, :])
            inner = jnp.sum(grad_probs * probs, axis=1, keepdims=True)
            grad_scores = (probs * (grad_probs - inner)).astype(jnp.bfloat16)
            grad_q = dot_plain(grad_scores, k_s[0:columns, :]) * scale
            grad_q = grad_q * cosine - pltpu.roll(grad_q, HEAD_DIM // 2, 1) * sine
            store_relative(
                order_ref, out_ref, piece, start, head * HEAD_DIM, grad_q.astype(jnp.bfloat16)
            )
            dk_s[0:columns, :] += dot_columns(grad_scores, q_blk)
            dv_s[0:columns, :] += dot_columns(probs.astype(jnp.bfloat16), g_blk)
    for block in range(length // BLOCK):
        start = block * BLOCK
        rows = slice(start, start + BLOCK)
        grad_k = dk_s[rows, :] * scale
        grad_k = grad_k * cos_ref[rows, :] - pltpu.roll(grad_k, HEAD_DIM // 2, 1) * sin_ref[rows, :]
        store_relative(order_ref, out_ref, piece, start, q_width, grad_k.astype(jnp.bfloat16))
        store_relative(
            order_ref,
            out_ref,
            piece,
            start,
            q_width + HEAD_DIM,
            dv_s[rows, :].astype(jnp.bfloat16),
        )


def head_spread(width):
    heads = iota_of((LANES, width), 0)
    return (iota_of((LANES, width), 1) // SSM_DIM == heads).astype(jnp.float32).astype(jnp.bfloat16)


def head_gather(width):
    heads = iota_of((width, LANES), 1)
    return (iota_of((width, LANES), 0) // SSM_DIM == heads).astype(jnp.float32).astype(jnp.bfloat16)


def triangle(lower):
    rows = iota_of((BLOCK, BLOCK), 0)
    columns = iota_of((BLOCK, BLOCK), 1)
    return (rows >= columns if lower else rows <= columns).astype(jnp.float32).astype(jnp.bfloat16)


def softplus(values):
    return jnp.maximum(values, 0.0) + jnp.log1p(jnp.exp(-jnp.abs(values)))


def mark_columns(marks_ref, row_start, first):
    return [
        jnp.broadcast_to(marks_ref[pl.ds(row_start, BLOCK), first + tap : first + tap + 1], (BLOCK, LANES))
        for tap in range(3)
    ]


def conv_window(pad_ref, taps_ref, before, row_start, column):
    total = jnp.broadcast_to(taps_ref[4:5, column : column + LANES], (BLOCK, LANES))
    shifted = []
    for tap in range(4):
        rows = pad_ref[column // LANES, pl.ds(row_start + 5 + tap, BLOCK), :]
        if tap < 3:
            rows = rows * before[tap]
        shifted.append(rows)
        total = total + rows * taps_ref[tap : tap + 1, column : column + LANES]
    return total, shifted


def mixer_load(
    x_column,
    order_ref,
    narrow_ref,
    bc_ref,
    marks_ref,
    x_taps_ref,
    bc_taps_ref,
    heads_ref,
    x_pad,
    bc_pad,
    dt_s,
    a_s,
    a_row_s,
    a_wide,
    mixed_s,
    scaled_s,
    bc_s,
):
    length, width = mixed_s.shape
    count, _, bc_width = bc_ref.shape
    pieces = 2 * count
    piece = length // pieces
    dt_column = narrow_ref.shape[1] - LANES
    x_pad[:, 0:8, :] = jnp.zeros((width // LANES, 8, LANES), jnp.float32)
    bc_pad[:, 0:8, :] = jnp.zeros((2 * STATE // LANES, 8, LANES), jnp.float32)
    for place in range(pieces):
        start = pl.multiple_of(order_ref[place] * piece, piece)
        rows = slice(place * piece, (place + 1) * piece)
        padded = slice(8 + place * piece, 8 + (place + 1) * piece)
        for chunk in range(width // LANES):
            column = x_column + chunk * LANES
            x_pad[chunk, padded, :] = narrow_ref[
                pl.ds(start, piece), column : column + LANES
            ].astype(jnp.float32)
        for owner in range(count):
            source = order_ref[pieces + owner]
            owner_start = pl.multiple_of(
                order_ref[pieces + count + owner * pieces + place] * piece, piece
            )
            lane = owner * bc_width % LANES
            bc_pad[owner * bc_width // LANES, padded, lane : lane + bc_width] = bc_ref[
                source, pl.ds(owner_start, piece), :
            ].astype(jnp.float32)
        dt_s[rows, :] = narrow_ref[pl.ds(start, piece), dt_column : dt_column + LANES].astype(
            jnp.float32
        )
    spread = head_spread(width)
    lower = triangle(True)
    rate = jnp.exp(heads_ref[0:1, :])
    bias = heads_ref[1:2, :]

    def one_block(block, carry):
        start = pl.multiple_of(block * BLOCK, BLOCK)
        rows = pl.ds(start, BLOCK)
        step = softplus(dt_s[rows, :] + bias)
        decay_sum = ones_dot(lower, step * rate, 3) + carry
        a_s[rows, :] = decay_sum
        a_row_s[block] = decay_sum.T
        a_wide[rows, :] = dot_ones(decay_sum, spread, 3)
        step_wide = dot_ones(step, spread, 2)
        before = mark_columns(marks_ref, start, 1)
        for column in range(0, width, LANES):
            lanes = slice(column, column + LANES)
            total, _ = conv_window(x_pad, x_taps_ref, before, start, column)
            mixed = total * logistic(total)
            mixed_s[rows, lanes] = mixed
            scaled_s[rows, lanes] = (mixed * step_wide[:, lanes]).astype(jnp.bfloat16)
        for column in range(0, 2 * STATE, LANES):
            total, _ = conv_window(bc_pad, bc_taps_ref, before, start, column)
            bc_s[rows, column : column + LANES] = (total * logistic(total)).astype(
                jnp.bfloat16
            )
        return decay_sum[BLOCK - 1 : BLOCK, :]

    lax.fori_loop(0, length // BLOCK, one_block, jnp.zeros((1, LANES), jnp.float32))


def half_lanes(values, half):
    lane = iota_of(values.shape, 1)
    keep = lane < SSM_DIM if half == 0 else lane >= SSM_DIM
    return jnp.where(keep, values, jnp.zeros_like(values))


def diagonal_decay(a_s, a_row_s, block, start, head):
    gap = a_row_s[block, head : head + 1, :] - a_s[pl.ds(start, BLOCK), head : head + 1]
    return jnp.exp(jnp.minimum(gap, 0.0))


def mixer_forward_kernel(
    x_column,
    order_ref,
    narrow_ref,
    bc_ref,
    marks_ref,
    seg_row_ref,
    x_taps_ref,
    bc_taps_ref,
    heads_ref,
    out_ref,
    x_pad,
    bc_pad,
    dt_s,
    a_s,
    a_row_s,
    a_wide,
    mixed_s,
    scaled_s,
    bc_s,
    weight_s,
    inter_s,
    total_s,
):
    length, width = mixed_s.shape
    piece = length // (2 * bc_ref.shape[0])
    mixer_load(
        x_column,
        order_ref,
        narrow_ref,
        bc_ref,
        marks_ref,
        x_taps_ref,
        bc_taps_ref,
        heads_ref,
        x_pad,
        bc_pad,
        dt_s,
        a_s,
        a_row_s,
        a_wide,
        mixed_s,
        scaled_s,
        bc_s,
    )
    skip_wide = dot_ones(jnp.broadcast_to(heads_ref[2:3, :], (8, LANES)), head_spread(width), 3)

    def one_block(block, _):
        start = pl.multiple_of(block * BLOCK, BLOCK)
        rows = pl.ds(start, BLOCK)
        out_c = bc_s[rows, STATE : 2 * STATE]
        total_s[...] = jnp.zeros_like(total_s)
        first = a_wide[pl.ds(start, 8), :][0:1]

        def earlier(other, _):
            col_start = pl.multiple_of(other * BLOCK, BLOCK)
            columns = pl.ds(col_start, BLOCK)
            allowed = allowed_block(marks_ref, seg_row_ref, start, col_start, BLOCK, False)
            inter = dot_rows(out_c, bc_s[columns, 0:STATE])
            inter = jnp.where(allowed, inter, 0.0).astype(jnp.bfloat16)
            faded = scaled_s[columns, :].astype(jnp.float32) * jnp.exp(a_wide[columns, :] - first)
            total_s[...] += dot_plain(inter, faded.astype(jnp.bfloat16))
            return 0

        lax.fori_loop(0, block, earlier, 0)
        allowed = allowed_block(marks_ref, seg_row_ref, start, start, BLOCK, True)
        inter_s[...] = jnp.where(allowed, dot_rows(out_c, bc_s[rows, 0:STATE]), 0.0)
        for column in range(0, width, LANES):
            lanes = slice(column, column + LANES)
            scaled = scaled_s[rows, lanes]
            mixed = total_s[:, lanes] * jnp.exp(first[:, lanes] - a_wide[rows, lanes])
            for half in range(2):
                head = column // SSM_DIM + half
                decay = diagonal_decay(a_s, a_row_s, block, start, head)
                weights = (inter_s[...] * decay).astype(jnp.bfloat16)
                mixed = mixed + dot_plain(weights, half_lanes(scaled, half))
            mixed = mixed + skip_wide[0:1, lanes] * mixed_s[rows, lanes]
            weight_s[:, lanes] = mixed.astype(jnp.bfloat16)
        for part in range(BLOCK // piece):
            place = block * (BLOCK // piece) + part
            target = pl.multiple_of(order_ref[place] * piece, piece)
            out_ref[pl.ds(target, piece), :] = weight_s[part * piece : (part + 1) * piece, :]
        return 0

    lax.fori_loop(0, length // BLOCK, one_block, 0)


def mixer_backward_kernel(
    x_column,
    order_ref,
    narrow_ref,
    bc_ref,
    grad_ref,
    marks_ref,
    seg_row_ref,
    x_taps_ref,
    bc_taps_ref,
    heads_ref,
    gx_ref,
    gdt_ref,
    gbc_ref,
    gx_taps_ref,
    gbc_taps_ref,
    gheads_ref,
    x_pad,
    bc_pad,
    dt_s,
    a_s,
    a_row_s,
    a_wide,
    mixed_s,
    scaled_s,
    bc_s,
    grad_s,
    gscaled_s,
    gap_s,
    gbc_s,
    inter_s,
    gover_s,
    faded_s,
    gfaded_s,
    fade_s,
    edge_s,
    ahead_s,
    low_s,
):
    length, width = mixed_s.shape
    count, _, bc_width = bc_ref.shape
    pieces = 2 * count
    piece = length // pieces
    blocks = length // BLOCK
    mixer_load(
        x_column,
        order_ref,
        narrow_ref,
        bc_ref,
        marks_ref,
        x_taps_ref,
        bc_taps_ref,
        heads_ref,
        x_pad,
        bc_pad,
        dt_s,
        a_s,
        a_row_s,
        a_wide,
        mixed_s,
        scaled_s,
        bc_s,
    )
    for place in range(pieces):
        source = pl.multiple_of(order_ref[place] * piece, piece)
        grad_s[place * piece : (place + 1) * piece, :] = grad_ref[pl.ds(source, piece), :]
    gscaled_s[...] = jnp.zeros_like(gscaled_s)
    gap_s[...] = jnp.zeros_like(gap_s)
    gbc_s[...] = jnp.zeros_like(gbc_s)

    def one_block(block, _):
        start = pl.multiple_of(block * BLOCK, BLOCK)
        rows = pl.ds(start, BLOCK)
        out_c = bc_s[rows, STATE : 2 * STATE]
        allowed = allowed_block(marks_ref, seg_row_ref, start, start, BLOCK, True)
        inter_s[...] = jnp.where(allowed, dot_rows(out_c, bc_s[rows, 0:STATE]), 0.0)
        gover_s[...] = jnp.zeros_like(gover_s)
        for column in range(0, width, LANES):
            lanes = slice(column, column + LANES)
            scaled = scaled_s[rows, lanes]
            grad = grad_s[rows, lanes]
            row_side = jnp.zeros((BLOCK, LANES), jnp.float32)
            col_side = jnp.zeros((BLOCK, LANES), jnp.float32)
            for half in range(2):
                head = column // SSM_DIM + half
                decay = diagonal_decay(a_s, a_row_s, block, start, head)
                weights = (inter_s[...] * decay).astype(jnp.bfloat16)
                scaled_half = half_lanes(scaled, half)
                gover_s[...] += dot_rows(grad, scaled_half) * decay
                row_side = row_side + dot_plain(weights, scaled_half)
                col_side = col_side + dot_columns(weights, half_lanes(grad, half))
            gscaled_s[rows, lanes] += col_side
            gap_s[rows, lanes] += scaled.astype(jnp.float32) * col_side - grad.astype(
                jnp.float32
            ) * row_side
        gover = jnp.where(allowed, gover_s[...], 0.0).astype(jnp.bfloat16)
        gbc_s[rows, STATE : 2 * STATE] += dot_plain(gover, bc_s[rows, 0:STATE])
        gbc_s[rows, 0:STATE] += dot_columns(gover, out_c)
        first = a_wide[pl.ds(start, 8), :][0:1]
        gfaded_s[...] = (
            grad_s[rows, :].astype(jnp.float32) * jnp.exp(first - a_wide[rows, :])
        ).astype(jnp.bfloat16)

        def earlier(other, _):
            col_start = pl.multiple_of(other * BLOCK, BLOCK)
            columns = pl.ds(col_start, BLOCK)
            same = allowed_block(marks_ref, seg_row_ref, start, col_start, BLOCK, False)
            in_b = bc_s[columns, 0:STATE]
            inter = jnp.where(same, dot_rows(out_c, in_b), 0.0).astype(jnp.bfloat16)
            fade_s[...] = jnp.exp(a_wide[columns, :] - first)
            faded_s[...] = (scaled_s[columns, :].astype(jnp.float32) * fade_s[...]).astype(
                jnp.bfloat16
            )
            over = dot_rows(gfaded_s[...], faded_s[...])
            over = jnp.where(same, over, 0.0).astype(jnp.bfloat16)
            gbc_s[rows, STATE : 2 * STATE] += dot_plain(over, in_b)
            gbc_s[columns, 0:STATE] += dot_columns(over, out_c)
            gap_s[rows, :] -= gfaded_s[...].astype(jnp.float32) * dot_plain(inter, faded_s[...])
            col_side = dot_columns(inter, gfaded_s[...])
            gap_s[columns, :] += faded_s[...].astype(jnp.float32) * col_side
            gscaled_s[columns, :] += fade_s[...] * col_side
            return 0

        lax.fori_loop(0, block, earlier, 0)
        return 0

    lax.fori_loop(0, blocks, one_block, 0)

    spread = head_spread(width)
    gather = head_gather(width)
    upper = triangle(False)
    rate = jnp.exp(heads_ref[0:1, :])
    bias = heads_ref[1:2, :]
    skip_wide = dot_ones(jnp.broadcast_to(heads_ref[2:3, :], (8, LANES)), spread, 3)
    gx_taps_ref[...] = jnp.zeros_like(gx_taps_ref)
    gbc_taps_ref[...] = jnp.zeros_like(gbc_taps_ref)
    gheads_ref[...] = jnp.zeros_like(gheads_ref)
    edge_s[...] = jnp.zeros_like(edge_s)

    def conv_back(pad_ref, taps_ref, gtaps_ref, before, after, start, column, shift, gmixed):
        total, shifted = conv_window(pad_ref, taps_ref, before, start, column)
        sig = logistic(total)
        gtotal = gmixed * sig * (1.0 + total * (1.0 - sig))
        lanes = slice(column, column + LANES)
        for tap in range(4):
            gtaps_ref[tap : tap + 1, lanes] += jnp.sum(gtotal * shifted[tap], axis=0, keepdims=True)
        gtaps_ref[4:5, lanes] += jnp.sum(gtotal, axis=0, keepdims=True)
        wide = slice(shift + column, shift + column + LANES)
        chunk = (shift + column) // LANES
        ahead_s[chunk, 0:BLOCK, :] = gtotal
        ahead_s[chunk, BLOCK : BLOCK + 8, :] = edge_s[:, wide]
        edge_s[:, wide] = gtotal[0:8]
        result = gtotal * taps_ref[3:4, lanes]
        for tap in range(3):
            ahead = ahead_s[chunk, 3 - tap : 3 - tap + BLOCK, :] * after[tap]
            result = result + ahead * taps_ref[tap : tap + 1, lanes]
        return result.astype(jnp.bfloat16)

    def last_block(index, carry):
        block = blocks - 1 - index
        start = pl.multiple_of(block * BLOCK, BLOCK)
        rows = pl.ds(start, BLOCK)
        raw = dt_s[rows, :] + bias
        step = softplus(raw)
        gsum = ones_dot(upper, dot_ones(gap_s[rows, :], gather, 2), 3) + carry
        gstep = dot_ones(gscaled_s[rows, :] * mixed_s[rows, :], gather, 2) + gsum * rate
        graw = gstep * jax.nn.sigmoid(raw)
        gheads_ref[0:1, :] += jnp.sum(gsum * step * rate, axis=0, keepdims=True)
        gheads_ref[1:2, :] += jnp.sum(graw, axis=0, keepdims=True)
        low_s[:, width : width + LANES] = graw.astype(jnp.bfloat16)
        step_wide = dot_ones(step, spread, 2)
        skip_parts = []
        before = mark_columns(marks_ref, start, 1)
        after = mark_columns(marks_ref, start, 4)
        for column in range(0, width, LANES):
            lanes = slice(column, column + LANES)
            grad = grad_s[rows, lanes].astype(jnp.float32)
            skip_parts.append(jnp.sum(grad * mixed_s[rows, lanes], axis=0, keepdims=True))
            gmixed = skip_wide[0:1, lanes] * grad + gscaled_s[rows, lanes] * step_wide[:, lanes]
            low_s[:, lanes] = conv_back(
                x_pad, x_taps_ref, gx_taps_ref, before, after, start, column, 0, gmixed
            )
        skip_row = jnp.broadcast_to(jnp.concatenate(skip_parts, axis=1), (8, width))
        gheads_ref[2:3, :] += dot_ones(skip_row, gather, 2)[0:1]
        for column in range(0, 2 * STATE, LANES):
            lanes = slice(column, column + LANES)
            low_s[:, width + LANES + column : width + 2 * LANES + column] = conv_back(
                bc_pad,
                bc_taps_ref,
                gbc_taps_ref,
                before,
                after,
                start,
                column,
                width,
                gbc_s[rows, lanes],
            )
        for part in range(BLOCK // piece):
            place = block * (BLOCK // piece) + part
            target = pl.multiple_of(order_ref[place] * piece, piece)
            gx_ref[pl.ds(target, piece), :] = low_s[part * piece : (part + 1) * piece, 0:width]
            gdt_ref[pl.ds(target, piece), :] = low_s[
                part * piece : (part + 1) * piece, width : width + LANES
            ]
            for owner in range(count):
                first = width + LANES + owner * bc_width
                owner_start = pl.multiple_of(
                    order_ref[pieces + count + owner * pieces + place] * piece, piece
                )
                gbc_ref[order_ref[pieces + owner], pl.ds(owner_start, piece), :] = low_s[
                    part * piece : (part + 1) * piece, first : first + bc_width
                ]
        return gsum[0:1, :]

    lax.fori_loop(0, blocks, last_block, jnp.zeros((1, LANES), jnp.float32))


def local_call(kernel, outs, scratch, flops, operands):
    moved = sum(part.size * part.dtype.itemsize for part in operands)
    moved += sum(part.size * part.dtype.itemsize for part in outs)
    return pl.pallas_call(
        kernel,
        out_shape=outs,
        in_specs=[pl.BlockSpec(memory_space=pltpu.SMEM)]
        + [pl.BlockSpec(memory_space=pltpu.VMEM)] * (len(operands) - 1),
        out_specs=[pl.BlockSpec(memory_space=pltpu.VMEM)] * len(outs),
        scratch_shapes=scratch,
        compiler_params=pltpu.CompilerParams(vmem_limit_bytes=KERNEL_VMEM),
        cost_estimate=pl.CostEstimate(flops=flops, bytes_accessed=moved, transcendentals=0),
    )(*operands)


def array_of(shape, dtype):
    return jax.ShapeDtypeStruct(shape, dtype)


def attention_forward(q_width, pieces, order, narrow, cosine, sine, marks, seg_row):
    length = narrow.shape[0]
    low = jnp.bfloat16
    return local_call(
        functools.partial(attention_forward_kernel, q_width, pieces),
        [array_of((length, q_width), low), array_of((length, 8), jnp.float32)],
        [
            pltpu.VMEM((length, q_width), low),
            pltpu.VMEM((length, HEAD_DIM), low),
            pltpu.VMEM((length, HEAD_DIM), low),
        ],
        36 * length * length * q_width,
        (order, narrow, cosine, sine, marks, seg_row),
    )


def attention_backward(q_width, pieces, order, narrow, grad, cosine, sine, marks, seg_row, lse):
    length = narrow.shape[0]
    low = jnp.bfloat16
    return local_call(
        functools.partial(attention_backward_kernel, q_width, pieces),
        [array_of((length, q_width + 2 * HEAD_DIM), low)],
        [
            pltpu.VMEM((length, q_width), low),
            pltpu.VMEM((length, HEAD_DIM), low),
            pltpu.VMEM((length, HEAD_DIM), low),
            pltpu.VMEM((length, q_width), low),
            pltpu.VMEM((length, HEAD_DIM), jnp.float32),
            pltpu.VMEM((length, HEAD_DIM), jnp.float32),
        ],
        44 * length * length * q_width,
        (order, narrow, grad, cosine, sine, marks, seg_row, lse),
    )[0]


def mixer_scratch(length, width):
    low, full = jnp.bfloat16, jnp.float32
    return [
        pltpu.VMEM((width // LANES, length + 8, LANES), full),
        pltpu.VMEM((2 * STATE // LANES, length + 8, LANES), full),
        pltpu.VMEM((length, LANES), full),
        pltpu.VMEM((length, LANES), full),
        pltpu.VMEM((length // BLOCK, LANES, BLOCK), full),
        pltpu.VMEM((length, width), full),
        pltpu.VMEM((length, width), full),
        pltpu.VMEM((length, width), low),
        pltpu.VMEM((length, 2 * STATE), low),
    ]


def mixer_forward(x_column, width, order, narrow, bc, marks, seg_row, x_taps, bc_taps, heads):
    length = narrow.shape[0]
    low, full = jnp.bfloat16, jnp.float32
    return local_call(
        functools.partial(mixer_forward_kernel, x_column),
        [array_of((length, width), low)],
        mixer_scratch(length, width)
        + [
            pltpu.VMEM((BLOCK, width), low),
            pltpu.VMEM((BLOCK, BLOCK), full),
            pltpu.VMEM((BLOCK, width), full),
        ],
        28 * length * length * width,
        (order, narrow, bc, marks, seg_row, x_taps, bc_taps, heads),
    )[0]


def mixer_backward(x_column, width, order, narrow, bc, grad, marks, seg_row, x_taps, bc_taps, heads):
    length = narrow.shape[0]
    low, full = jnp.bfloat16, jnp.float32
    return local_call(
        functools.partial(mixer_backward_kernel, x_column),
        [
            array_of((length, width), low),
            array_of((length, LANES), low),
            array_of(bc.shape, low),
            array_of((8, width), full),
            array_of((8, 2 * STATE), full),
            array_of((8, LANES), full),
        ],
        mixer_scratch(length, width)
        + [
            pltpu.VMEM((length, width), low),
            pltpu.VMEM((length, width), full),
            pltpu.VMEM((length, width), full),
            pltpu.VMEM((length, 2 * STATE), full),
            pltpu.VMEM((BLOCK, BLOCK), full),
            pltpu.VMEM((BLOCK, BLOCK), full),
            pltpu.VMEM((BLOCK, width), low),
            pltpu.VMEM((BLOCK, width), low),
            pltpu.VMEM((BLOCK, width), full),
            pltpu.VMEM((8, width + 2 * STATE), full),
            pltpu.VMEM(((width + 2 * STATE) // LANES, BLOCK + 8, LANES), full),
            pltpu.VMEM((BLOCK, width + LANES + 2 * STATE), low),
        ],
        60 * length * length * width,
        (order, narrow, bc, grad, marks, seg_row, x_taps, bc_taps, heads),
    )


def document_marks(seg_row):
    length = seg_row.shape[0]
    before = jnp.pad(seg_row, (3, 0), constant_values=-1)
    after = jnp.pad(seg_row, (0, 3), constant_values=-1)
    columns = [seg_row.astype(jnp.float32)]
    for tap in range(3):
        columns.append((before[tap : tap + length] == seg_row).astype(jnp.float32))
    for tap in range(3):
        columns.append((after[3 - tap : 3 - tap + length] == seg_row).astype(jnp.float32))
    columns.append(jnp.zeros((length,), jnp.float32))
    return jnp.stack(columns, axis=1)


def rope_wide(length):
    half_dim = HEAD_DIM // 2
    frequency = rope_base ** (-jnp.arange(half_dim, dtype=jnp.float32) / half_dim)
    angles = jnp.arange(length, dtype=jnp.float32)[:, None] * frequency[None, :]
    cosine, sine = jnp.cos(angles), jnp.sin(angles)
    return jnp.concatenate([cosine, cosine], axis=1), jnp.concatenate([-sine, sine], axis=1)


def swap_seq(value, bit, count):
    return lax.ppermute(value, "seq", [(place, place ^ bit) for place in range(count)])


def seq_bits(count):
    bits = []
    bit = 1
    while bit < count:
        bits.append(bit)
        bit *= 2
    return bits


def block_order(bits):
    order = [0]
    for bit in bits:
        order = order + [place ^ bit for place in order]
    return order


def relative_order(count):
    bits = seq_bits(count)
    upper = [(0, block) for block in block_order(bits)]
    lower = [(1, block) for block in block_order(bits[::-1])]
    near = count // 2
    return upper[:near] + lower[:near] + upper[near:] + lower[near:]


def gather_first(rows, count):
    half = rows.shape[0] // 2
    bits = seq_bits(count)
    pieces = []
    for piece, order in ((rows[:half], bits), (rows[half:], bits[::-1])):
        for bit in order[:-1]:
            piece = jnp.concatenate([piece, swap_seq(piece, bit, count)], axis=0)
        pieces.append(piece)
    return pieces


def gather_last(pieces, count):
    bits = seq_bits(count)
    far = [swap_seq(piece, bit, count) for piece, bit in zip(pieces, (bits[-1], bits[0]))]
    return jnp.concatenate(pieces, axis=0), jnp.concatenate(far, axis=0)


def rows_gather(rows, count):
    return gather_last(gather_first(rows, count), count)


def scatter_first(far, count):
    half = far.shape[0] // 2
    bits = seq_bits(count)
    far = far.astype(jnp.bfloat16)
    return [
        swap_seq(far[first : first + half], order[-1], count)
        for first, order in ((0, bits), (half, bits[::-1]))
    ]


def scatter_second(near, came, count):
    half = near.shape[0] // 2
    bits = seq_bits(count)
    kept, arrived = [], []
    for first, order, add in ((0, bits, came[0]), (half, bits[::-1], came[1])):
        piece = near[first : first + half]
        for bit in order[:-1][::-1]:
            piece = piece + add.astype(jnp.float32)
            keep = piece.shape[0] // 2
            add = swap_seq(piece[keep:].astype(jnp.bfloat16), bit, count)
            piece = piece[:keep]
        kept.append(piece)
        arrived.append(add)
    return kept, arrived


def scatter_last(kept, arrived):
    return jnp.concatenate(
        [piece + add.astype(jnp.float32) for piece, add in zip(kept, arrived)], axis=0
    )


def rows_scatter(near, far, count):
    came = scatter_first(far, count)
    return scatter_last(*scatter_second(near, came, count))


def row_tables(count):
    order = relative_order(count)

    def places(rank):
        return [order.index((half, block ^ rank)) for block in range(count) for half in range(2)]

    everyone = [place for rank in range(count) for place in places(rank)]
    return np.asarray(
        [
            places(rank) + [other ^ rank for other in range(count)] + everyone
            for rank in range(count)
        ],
        np.int32,
    )


def seq_pieces(value, count):
    return [value] + [swap_seq(value, bit, count) for bit in range(1, count)]


def seq_sum(value, count):
    order = relative_order(count)
    total = value.reshape(2 * count, -1)
    for bit in range(1, count):
        came = swap_seq(value, bit, count).reshape(2 * count, -1)
        places = [order.index((half, block ^ bit)) for half, block in order]
        total = total + jnp.concatenate([came[place : place + 1] for place in places])
    return total.reshape(-1)


def norm_forward(rows, gain):
    scale = lax.rsqrt(jnp.mean(rows * rows, axis=-1, keepdims=True) + epsilon)
    return ((rows * scale * gain).astype(jnp.bfloat16), scale)


def norm_backward(rows, scale, gain, cotangent):
    weighted = cotangent * gain
    inner = jnp.mean(rows * weighted, axis=-1, keepdims=True)
    grad_rows = scale * weighted - rows * (scale * scale * scale * inner)
    return grad_rows


def columns_exchange(blocks):
    return lax.all_to_all(blocks, "seq", split_axis=0, concat_axis=0, tiled=True)


def rows_of_all(piece):
    return lax.all_gather(piece, "fsdp", axis=1, tiled=True).reshape(-1, piece.shape[2])


def columns_gather(blocks):
    return rows_of_all(columns_exchange(blocks))


def columns_to_owners(blocks):
    blocks = with_layout_constraint(blocks, Layout(major_to_minor=(0, 1, 2)))
    return lax.all_to_all(blocks, "seq", split_axis=0, concat_axis=0, tiled=True)


def rank_parts(arrived):
    return [arrived[place].astype(jnp.float32) for place in range(arrived.shape[0])]


def side_by_side(parts, first, width):
    return jnp.concatenate([part[:, first : first + width] for part in parts], axis=1)


def body(
    seq_count,
    fsdp_count,
    hidden_in,
    segments,
    out_grad,
    norm1_gain,
    w_query,
    w_keyval,
    w_attn_out,
    w_gate_z,
    w_ssm_x,
    w_ssm_bc,
    w_ssm_dt,
    conv_taps,
    a_log,
    dt_bias,
    skip_gain,
    ssm_gain,
    w_ssm_out,
    norm2_gain,
    w_ff_gate,
    w_ff_up,
    w_ff_down,
):
    f32, bf16 = jnp.float32, jnp.bfloat16
    batch, block_len, model_width = hidden_in.shape
    length = block_len * seq_count
    rank = lax.axis_index("seq")
    seg_row = segments[0]
    heads_local = HEADS // seq_count
    group_size = HEADS // KV_HEADS
    q_width = w_query.shape[1] // seq_count
    z_width = w_gate_z.shape[1] // seq_count
    x_width = w_ssm_x.shape[1] // seq_count
    bc_width = w_ssm_bc.shape[1] // seq_count
    dt_width = w_ssm_dt.shape[1] // seq_count
    ff_width = w_ff_gate.shape[1] // seq_count
    kv_total = w_keyval.shape[1] // 2
    heads_total = a_log.shape[0]
    dssm = w_ssm_x.shape[1]
    row_piece = w_query.shape[0]
    bc_pad = -bc_width % LANES
    dt_pad = -dt_width % LANES

    def pack(vector):
        parts = -(-vector.shape[0] // row_piece)
        padded = jnp.pad(vector, (0, parts * row_piece - vector.shape[0]))
        return [padded[part * row_piece : (part + 1) * row_piece] for part in range(parts)]

    def unpack(columns, length_each):
        spread = columns.reshape(columns.shape[0], -1, row_piece).transpose(1, 0, 2)
        return spread.reshape(spread.shape[0], -1)[:, :length_each].reshape(-1)

    extra_columns = [norm1_gain, norm2_gain] + pack(ssm_gain)
    ssm_pieces = len(extra_columns) - 2
    for tap in range(conv_taps.shape[1]):
        extra_columns += pack(conv_taps[:, tap])
    taps_pieces = (len(extra_columns) - 2 - ssm_pieces) // conv_taps.shape[1]
    extra_block = jnp.pad(
        jnp.stack(extra_columns, axis=1), ((0, 0), (0, dt_pad - len(extra_columns)))
    )
    free_first = q_width + 2 * HEAD_DIM + x_width + bc_width + bc_pad + dt_width
    sends = []
    for target in range(seq_count):
        kv_head = target * heads_local // group_size
        sends.append(
            jnp.concatenate(
                [
                    w_query[:, target * q_width : (target + 1) * q_width],
                    w_keyval[:, kv_head * HEAD_DIM : (kv_head + 1) * HEAD_DIM],
                    w_keyval[:, kv_total + kv_head * HEAD_DIM : kv_total + (kv_head + 1) * HEAD_DIM],
                    w_ssm_x[:, target * x_width : (target + 1) * x_width],
                    w_ssm_bc[:, target * bc_width : (target + 1) * bc_width],
                    jnp.zeros((row_piece, bc_pad), bf16),
                    w_ssm_dt[:, target * dt_width : (target + 1) * dt_width],
                    extra_block,
                ],
                axis=1,
            )
        )
    narrow_piece = columns_exchange(jnp.stack(sends))
    narrow_w = rows_of_all(narrow_piece)
    extras = lax.slice_in_dim(narrow_w, free_first, free_first + len(extra_columns), axis=1).T
    extras = extras.astype(f32)
    gain1, gain2 = extras[0], extras[1]
    taps_rows, taps_width = conv_taps.shape
    ssm_count = ssm_gain.shape[0]
    gain_ssm = unpack(extras[2 : 2 + ssm_pieces], ssm_count)
    gain_ssm = lax.dynamic_slice_in_dim(gain_ssm, rank * z_width, z_width, 0)
    taps = [
        unpack(extras[first : first + taps_pieces], taps_rows)
        for first in range(2 + ssm_pieces, len(extra_columns), taps_pieces)
    ]
    taps_rows8 = jnp.pad(jnp.stack(taps), ((0, 8 - taps_width), (0, 0)))
    x_taps = lax.dynamic_slice_in_dim(taps_rows8, rank * x_width, x_width, 1)
    bc_taps = taps_rows8[:, dssm:]
    head_rows = lax.dynamic_slice_in_dim(
        jnp.stack([a_log, dt_bias, skip_gain]), rank * dt_width, dt_width, 1
    )
    head_rows = jnp.pad(head_rows, ((0, 5), (0, dt_pad)))
    marks = document_marks(seg_row)
    seg_line = jnp.broadcast_to(seg_row.astype(f32)[None, :], (8, length))

    to_true = lax.dynamic_index_in_dim(jnp.asarray(row_tables(seq_count)), rank, 0, False)
    pieces = 2 * seq_count

    own_in = hidden_in.reshape(block_len, model_width)
    narrow_piece, own_in = lax.optimization_barrier((narrow_piece, own_in))
    all_in = jnp.concatenate(rows_gather(own_in, seq_count), axis=0)
    all_in, w_gate_z, w_ff_gate, w_ff_up, w_attn_out, w_ssm_out = lax.optimization_barrier(
        (all_in, w_gate_z, w_ff_gate, w_ff_up, w_attn_out, w_ssm_out)
    )
    wide_piece = columns_exchange(
        jnp.stack(
            [
                jnp.concatenate(
                    [
                        w_gate_z[:, target * z_width : (target + 1) * z_width],
                        w_ff_gate[:, target * ff_width : (target + 1) * ff_width],
                        w_ff_up[:, target * ff_width : (target + 1) * ff_width],
                    ],
                    axis=1,
                )
                for target in range(seq_count)
            ]
        )
    )
    z_piece, ff_piece = wide_piece[:, :, :z_width], wide_piece[:, :, z_width:]
    z_w = rows_of_all(z_piece)
    out_piece = jnp.concatenate([w_attn_out, w_ssm_out], axis=0)
    z_piece, out_piece = lax.optimization_barrier((z_piece, out_piece))
    out_w = lax.all_gather(out_piece, "fsdp", axis=0)

    cosine, sine = rope_wide(length)
    all_in, cosine, sine, marks, seg_line, to_true = lax.optimization_barrier(
        (all_in, cosine, sine, marks, seg_line, to_true)
    )
    ff_w = rows_of_all(ff_piece)
    normed, _ = norm_forward(all_in.astype(f32), gain1)
    edges = [0]
    for width in (q_width, HEAD_DIM, HEAD_DIM, x_width, bc_width + bc_pad, dt_width + dt_pad):
        edges.append(edges[-1] + width)
    narrow = mat_product(normed, narrow_w).astype(bf16)
    narrow, out_grad = lax.optimization_barrier((narrow, out_grad))
    grad_own = out_grad.reshape(block_len, model_width)
    grad_ff = gather_first(grad_own, seq_count)
    bc_seq = jnp.stack(seq_pieces(narrow[:, edges[4] : edges[4] + bc_width], seq_count))
    attn_rel, lse_seq = attention_forward(
        q_width, pieces, to_true, narrow, cosine, sine, marks, seg_line
    )
    bc_seq, attn_rel, w_ff_down, grad_ff = lax.optimization_barrier(
        (bc_seq, attn_rel, w_ff_down, grad_ff)
    )
    grad_ff = gather_last(grad_ff, seq_count)
    down_w = lax.all_gather(w_ff_down, "fsdp", axis=0, tiled=True)
    mixer_args = (x_taps, bc_taps, head_rows)
    ssm_rel = mixer_forward(
        edges[3], x_width, to_true, narrow, bc_seq, marks, seg_line, *mixer_args
    )
    ssm_rel, z_w, grad_ff = lax.optimization_barrier((ssm_rel, z_w, grad_ff))
    ssm_rel = ssm_rel.astype(f32)
    gate_z = mat_product(normed, z_w)
    gate_sig = jax.nn.sigmoid(gate_z)
    gate_silu = gate_z * gate_sig
    gated = ssm_rel * gate_silu
    square_sum = seq_sum(jnp.sum(gated * gated, axis=1), seq_count)
    gated_scale = lax.rsqrt(square_sum / dssm + epsilon)[:, None]
    ssm_in = (gated * gated_scale * gain_ssm).astype(bf16)
    ssm_in, out_w = lax.optimization_barrier((ssm_in, out_w))
    attn_out_w = out_w[:, : w_attn_out.shape[0]].reshape(-1, model_width)
    ssm_out_w = out_w[:, w_attn_out.shape[0] :].reshape(-1, model_width)
    near = length // 2

    def out_product(first):
        rows = slice(first, first + near)
        return mat_product(attn_rel[rows], attn_out_w) + mat_product(ssm_in[rows], ssm_out_w)

    xin = own_in.astype(f32)
    middle = xin + rows_scatter(out_product(0), out_product(near), seq_count)

    own_normed2, scale2 = norm_forward(middle, gain2)
    normed2 = rows_gather(own_normed2, seq_count)

    def ff_forward(rows):
        gate_ff = mat_product(rows, ff_w[:, :ff_width])
        up_ff = mat_product(rows, ff_w[:, ff_width:])
        ff_sig = jax.nn.sigmoid(gate_ff)
        ff_silu = gate_ff * ff_sig
        return up_ff, ff_sig, ff_silu, (ff_silu * up_ff).astype(bf16), gate_ff

    def ff_backward(grad_rows, up_ff, ff_sig, ff_silu):
        grad_act = input_grad(grad_rows, down_w)
        grad_gate_ff = grad_act * up_ff * (ff_sig + ff_silu * (1.0 - ff_sig))
        grad_up_ff = grad_act * ff_silu
        return jnp.concatenate([grad_gate_ff.astype(bf16), grad_up_ff.astype(bf16)], axis=1)

    up_near, sig_near, silu_near, act_near, gate_near = ff_forward(normed2[0])
    normed2_far, act_near, up_near, gate_near = lax.optimization_barrier(
        (normed2[1], act_near, up_near, gate_near)
    )
    sig_near = jax.nn.sigmoid(gate_near)
    silu_near = gate_near * sig_near
    up_far, sig_far, silu_far, act_far, gate_far = ff_forward(normed2_far)
    act = jnp.concatenate([act_near, act_far], axis=0)
    grad_ff_all = jnp.concatenate(grad_ff, axis=0)
    normed2_all = jnp.concatenate([normed2[0], normed2_far], axis=0)
    act, grad_ff_all = lax.optimization_barrier((act, grad_ff_all))
    grad_w_down = weight_grad(act, grad_ff_all).astype(bf16)
    grad_ff_far, grad_w_down = lax.optimization_barrier((grad_ff[1], grad_w_down))
    grad_w_down = lax.psum_scatter(grad_w_down, "fsdp", scatter_dimension=0, tiled=True)
    pair_far = ff_backward(grad_ff_far, up_far, sig_far, silu_far)
    pair_far = lax.optimization_barrier(pair_far)
    normed2_grad_far = input_grad(pair_far, ff_w).astype(bf16)
    grad_ff_near, normed2_grad_far = lax.optimization_barrier((grad_ff[0], normed2_grad_far))
    pair_near = ff_backward(grad_ff_near, up_near, sig_near, silu_near)
    pair_near = lax.optimization_barrier(pair_near)
    normed2_grad_near = input_grad(pair_near, ff_w)
    grad_pair = jnp.concatenate([pair_near, pair_far], axis=0)
    grad_pair, normed2_all = lax.optimization_barrier((grad_pair, normed2_all))
    grad_w_ff = weight_grad(normed2_all, grad_pair).astype(bf16)
    grad_w_ff = lax.psum_scatter(
        grad_w_ff.reshape(seq_count, -1, 2 * ff_width), "fsdp", scatter_dimension=1, tiled=True
    )
    grad_normed2 = rows_scatter(normed2_grad_near, normed2_grad_far, seq_count)
    grad_normed2, grad_w_down = lax.optimization_barrier((grad_normed2, grad_w_down))
    grad_middle_norm = norm_backward(middle, scale2, gain2, grad_normed2)
    grad_middle = grad_own.astype(f32) + grad_middle_norm

    mix_near, mix_far = rows_gather(grad_middle.astype(bf16), seq_count)
    ff_near = mat_product(act[:near], down_w)
    ff_far = mat_product(act[near:], down_w).astype(bf16)
    mix_far, ff_near, ff_far = lax.optimization_barrier((mix_far, ff_near, ff_far))
    grad_mix = jnp.concatenate([mix_near, mix_far], axis=0)
    grad_attn = input_grad(grad_mix, attn_out_w).astype(bf16)
    grad_ssm_in = input_grad(grad_mix, ssm_out_w)
    grad_w_attn = weight_grad(attn_rel, grad_mix).astype(bf16)
    grad_w_ssm = weight_grad(ssm_in, grad_mix).astype(bf16)
    weighted = grad_ssm_in * gain_ssm
    inner = seq_sum(jnp.sum(gated * weighted, axis=1), seq_count)
    out_grads = jnp.concatenate(
        [
            grad_w_attn.reshape(fsdp_count, -1, model_width),
            grad_w_ssm.reshape(fsdp_count, -1, model_width),
        ],
        axis=1,
    )
    grad_qkv = attention_backward(
        q_width, pieces, to_true, narrow, grad_attn, cosine, sine, marks, seg_line, lse_seq
    )
    inner, out_grads = lax.optimization_barrier((inner, out_grads))
    out_grads = lax.psum_scatter(out_grads, "fsdp", scatter_dimension=0, tiled=True)[0]
    inner = inner[:, None] / dssm
    grad_gated = gated_scale * weighted - gated * (
        gated_scale * gated_scale * gated_scale * inner
    )
    grad_ssm = (grad_gated * gate_silu).astype(bf16)
    grad_z = (grad_gated * ssm_rel * (gate_sig + gate_silu * (1.0 - gate_sig))).astype(bf16)
    grad_zq = lax.optimization_barrier(jnp.concatenate([grad_z, grad_qkv], axis=1))
    grad_w_zq = weight_grad(normed, grad_zq).astype(bf16)
    grad_ssm, grad_w_zq, ff_far, grad_w_ff = lax.optimization_barrier(
        (grad_ssm, grad_w_zq, ff_far, grad_w_ff)
    )
    grad_w_zq = lax.psum_scatter(
        grad_w_zq.reshape(seq_count, -1, grad_zq.shape[1]),
        "fsdp",
        scatter_dimension=1,
        tiled=True,
    )
    ff_came = scatter_first(ff_far, seq_count)
    grad_x, grad_dt, grad_bc_part, grad_x_taps, grad_bc_taps, grad_heads = mixer_backward(
        edges[3], x_width, to_true, narrow, bc_seq, grad_ssm, marks, seg_line, *mixer_args
    )
    grad_w_ff, grad_bc_part, ff_came = lax.optimization_barrier(
        (grad_w_ff, grad_bc_part, ff_came)
    )
    ff_cols = columns_to_owners(grad_w_ff)
    grad_bc = grad_bc_part[0].astype(f32)
    for bit in range(1, seq_count):
        grad_bc = grad_bc + swap_seq(grad_bc_part[bit], bit, seq_count).astype(f32)
    grad_bc = grad_bc.astype(bf16)
    ff_near, grad_bc = lax.optimization_barrier((ff_near, grad_bc))
    ff_kept, ff_arrived = scatter_second(ff_near, ff_came, seq_count)
    bc_zeros = jnp.zeros((length, bc_pad), bf16)
    grad_rest = jnp.concatenate([grad_x, grad_bc, bc_zeros, grad_dt], axis=1)
    grad_rest, out_grads, ff_cols = lax.optimization_barrier((grad_rest, out_grads, ff_cols))
    per_device = (seq_count, fsdp_count, -1)
    x_conv = lax.dynamic_update_slice_in_dim(
        jnp.zeros((dssm, taps_width), f32), grad_x_taps[:taps_width].T, rank * x_width, 0
    )
    conv_grads = jnp.concatenate([x_conv, grad_bc_taps[:taps_width].T], axis=0).reshape(per_device)
    head_grads = lax.dynamic_update_slice(
        jnp.zeros((3, heads_total), f32),
        grad_heads[:3, :dt_width],
        (jnp.int32(0), rank * dt_width),
    )
    head_grads = jnp.broadcast_to(
        head_grads.reshape(1, 1, -1), (seq_count, fsdp_count, 3 * heads_total)
    )
    smalls = jnp.concatenate([conv_grads, head_grads], axis=2)
    small_count = smalls.shape[2]
    small_columns = -(-small_count // row_piece)
    smalls = jnp.pad(smalls, ((0, 0), (0, 0), (0, small_columns * row_piece - small_count)))
    smalls = smalls.reshape(model_width, small_columns)
    small_first = x_width + bc_width + bc_pad + dt_width
    small_room = grad_rest.shape[1] - small_first - small_columns
    smalls = jnp.pad(smalls, ((0, 0), (small_first, small_room)))
    grad_w_rest = (weight_grad(normed, grad_rest) + smalls).astype(bf16)
    grad_rest, grad_w_rest, grad_z, grad_qkv, ff_arrived = lax.optimization_barrier(
        (grad_rest, grad_w_rest, grad_z, grad_qkv, ff_arrived)
    )
    grad_w_rest = lax.psum_scatter(
        grad_w_rest.reshape(seq_count, -1, grad_rest.shape[1]),
        "fsdp",
        scatter_dimension=1,
        tiled=True,
    )

    def first_product(first):
        rows = slice(first, first + near)
        return (
            input_grad(grad_rest[rows], narrow_w[:, edges[3] :])
            + input_grad(grad_z[rows], z_w)
            + input_grad(grad_qkv[rows], narrow_w[:, : edges[3]])
        )

    grad_normed_far = first_product(near).astype(bf16)
    zq_cols = columns_to_owners(grad_w_zq)
    grad_normed_far, grad_rest, grad_z, grad_qkv = lax.optimization_barrier(
        (grad_normed_far, grad_rest, grad_z, grad_qkv)
    )
    normed_came = scatter_first(grad_normed_far, seq_count)
    grad_normed_near, zq_cols = lax.optimization_barrier((first_product(0), zq_cols))
    normed_kept, normed_arrived = scatter_second(grad_normed_near, normed_came, seq_count)
    normed_kept, ff_kept, ff_cols, out_grads = lax.optimization_barrier(
        (normed_kept, ff_kept, ff_cols, out_grads)
    )
    layer_out = middle + scatter_last(ff_kept, ff_arrived)
    grad_normed = scatter_last(normed_kept, normed_arrived)
    _, scale1 = norm_forward(xin, gain1)
    grad_in_norm = norm_backward(xin, scale1, gain1, grad_normed)
    grad_in = (grad_middle + grad_in_norm).astype(bf16)
    grad_in, grad_w_rest = lax.optimization_barrier((grad_in, grad_w_rest))

    ff_cols = rank_parts(ff_cols)
    zq_cols = rank_parts(zq_cols)
    rest_cols = rank_parts(columns_to_owners(grad_w_rest))
    bc_first = x_width
    dt_first = bc_first + bc_width + bc_pad
    small = sum(part[:, small_first : small_first + small_columns] for part in rest_cols)
    small = small.reshape(-1)[:small_count]
    taps_total = taps_rows * taps_width
    out_conv = small[:taps_total]
    out_heads = small[taps_total:].reshape(3, heads_total)
    ranks_per_kv = group_size // heads_local
    kv_cols = []
    for first in (z_width + edges[1], z_width + edges[2]):
        for head in range(KV_HEADS):
            shares = zq_cols[head * ranks_per_kv : (head + 1) * ranks_per_kv]
            kv_cols.append(sum(share[:, first : first + HEAD_DIM] for share in shares))
    attn_rows = w_attn_out.shape[0]
    grad_query = side_by_side(zq_cols, z_width, q_width)
    grad_keyval = jnp.concatenate(kv_cols, axis=1)
    grad_gate_z = side_by_side(zq_cols, 0, z_width)
    grad_ssm_x = side_by_side(rest_cols, 0, x_width)
    grad_ssm_bc = side_by_side(rest_cols, bc_first, bc_width)
    grad_ssm_dt = side_by_side(rest_cols, dt_first, dt_width)
    grad_ff_gate = side_by_side(ff_cols, 0, ff_width)
    grad_ff_up = side_by_side(ff_cols, ff_width, ff_width)
    grad_attn_out = out_grads[:attn_rows].astype(f32)
    grad_ssm_out = out_grads[attn_rows:].astype(f32)

    def gain_grad(gain, *pairs):
        total = sum(jnp.sum(weight.astype(f32) * grad, axis=1) for weight, grad in pairs)
        return total / gain.astype(f32)

    out_gain1 = gain_grad(
        norm1_gain,
        (w_query, grad_query),
        (w_keyval, grad_keyval),
        (w_gate_z, grad_gate_z),
        (w_ssm_x, grad_ssm_x),
        (w_ssm_bc, grad_ssm_bc),
        (w_ssm_dt, grad_ssm_dt),
    )
    out_gain2 = gain_grad(norm2_gain, (w_ff_gate, grad_ff_gate), (w_ff_up, grad_ff_up))
    out_ssm_gain = gain_grad(ssm_gain, (w_ssm_out, grad_ssm_out))
    return (
        layer_out.astype(bf16).reshape(batch, block_len, model_width),
        grad_in.reshape(batch, block_len, model_width),
        out_gain1,
        grad_query,
        grad_keyval,
        grad_attn_out,
        grad_gate_z,
        grad_ssm_x,
        grad_ssm_bc,
        grad_ssm_dt,
        out_conv.reshape(taps_rows, taps_width),
        out_heads[0],
        out_heads[1],
        out_heads[2],
        out_ssm_gain,
        grad_ssm_out,
        out_gain2,
        grad_ff_gate,
        grad_ff_up,
        grad_w_down.astype(f32),
    )


def solution(mesh):
    in_specs = (
        P("fsdp", "seq", None),
        P("fsdp", None),
        P("fsdp", "seq", None),
        P(("seq", "fsdp")),
        P(("seq", "fsdp"), None),
        P(("seq", "fsdp"), None),
        P(("seq", "fsdp"), None),
        P(("seq", "fsdp"), None),
        P(("seq", "fsdp"), None),
        P(("seq", "fsdp"), None),
        P(("seq", "fsdp"), None),
        P(("seq", "fsdp"), None),
        P(),
        P(),
        P(),
        P(("seq", "fsdp")),
        P(("seq", "fsdp"), None),
        P(("seq", "fsdp")),
        P(("seq", "fsdp"), None),
        P(("seq", "fsdp"), None),
        P(("seq", "fsdp"), None),
    )
    out_specs = (
        P("fsdp", "seq", None),
        P("fsdp", "seq", None),
        P(("seq", "fsdp")),
        P(("seq", "fsdp"), None),
        P(("seq", "fsdp"), None),
        P(("seq", "fsdp"), None),
        P(("seq", "fsdp"), None),
        P(("seq", "fsdp"), None),
        P(("seq", "fsdp"), None),
        P(("seq", "fsdp"), None),
        P(("seq", "fsdp"), None),
        P(),
        P(),
        P(),
        P(("seq", "fsdp")),
        P(("seq", "fsdp"), None),
        P(("seq", "fsdp")),
        P(("seq", "fsdp"), None),
        P(("seq", "fsdp"), None),
        P(("seq", "fsdp"), None),
    )
    step = functools.partial(body, mesh.shape["seq"], mesh.shape["fsdp"])
    return jax.shard_map(step, mesh=mesh, in_specs=in_specs, out_specs=out_specs, check_vma=False)
```

profile of v0, /device:TPU:0, one launch (start us, length us, event | category | flops | bytes accessed | tf_op | source)
XLA Modules:
  0.0 651.3 jit_solution(11475172794299202746)
XLA Ops:
  15.3 16.4 %all_to_all.25 = bf16[4,64,1536]{2,1,0:T(8,128)(2,1)} all-to-all(bf16[4,64,1536]{2,1,0:T(8,128)(2,1)S(1)} %pad_maximum_fusion.26), channel_id=1, replica_groups=mesh['seq'=4,'fsdp'=8] {'seq'}, dimensions={0} | all-to-all | bytes 1572864 | tf_op jit(solution)/shard_map/all_to_all | solution.py:933
  33.5 10.6 %collective-permute-done = bf16[128,2048]{1,0:T(8,128)(2,1)S(1)} collective-permute-done((bf16[128,2048]{1,0:T(8,128)(2,1)S(1)}, bf16[128,2048]{1,0:T(8,128)(2,1)S(1)}, u32[]{:S(2)}, u32[]{:S(2)}) %collective-permute-start) | collective-permute-done | bytes 524320 | tf_op jit(solution)/shard_map/ppermute | solution.py:805
  46.5 21.1 %collective-permute-done.2 = bf16[256,2048]{1,0:T(8,128)(2,1)S(1)} collective-permute-done((bf16[256,2048]{1,0:T(8,128)(2,1)S(1)}, bf16[256,2048]{1,0:T(8,128)(2,1)S(1)}, u32[]{:S(2)}, u32[]{:S(2)}) %collective-permute-start.2) | collective-permute-done | bytes 1048608 | tf_op jit(solution)/shard_map/ppermute | solution.py:805
  70.7 18.3 %all_to_all.26 = bf16[4,64,2816]{2,1,0:T(8,128)(2,1)S(1)} all-to-all(bf16[4,64,2816]{2,1,0:T(8,128)(2,1)S(1)} %pad_maximum_fusion.14), channel_id=1, replica_groups=mesh['seq'=4,'fsdp'=8] {'seq'}, dimensions={0} | all-to-all | bytes 2883584 | tf_op jit(solution)/shard_map/all_to_all | solution.py:933
  103.8 11.0 %convolution_convert_fusion.2.narrow_ref = bf16[1024,1536]{1,0:T(8,128)(2,1)S(1)} fusion(bf16[2048,1536]{1,0:T(8,128)(2,1)} %bitcast.334, bf16[1024,2048]{1,0:T(8,128)(2,1)} %copy-done.25, f32[2048]{0:T(1024)S(1)} %bitcast.363, f32[1024]{0:T(1024)S(1)} %add_rsqrt_fusion), kind=kOutput, calls=%fused_computation.16 | convolution fusion | flops 6452412416 | bytes 13643776 | tf_op jit(solution)/shard_map/dot_general | solution.py:28
  120.7 7.7 %shard_map.365 = (bf16[1024,256]{1,0:T(8,128)(2,1)}, f32[1024,8]{1,0:T(8,128)}) custom-call(s32[44]{0:T(128)} %fusion.74.order_ref, bf16[1024,1536]{1,0:T(8,128)(2,1)} %copy-done.79, f32[1024,128]{1,0:T(8,128)} %get-tuple-element.112.cos_ref, f32[1024,128]{1,0:T(8,128)} %get-tuple-element.113.sin_ref, f32[1024,8]{1,0:T(8,128)} %copy.99.marks_ref, ...), custom_call_target="tpu_custom_call" | custom-call | flops 9663676416 | bytes 4817072 | tf_op jit(solution)/shard_map/pallas_call | solution.py:667
  141.6 19.4 %shard_map.366 = bf16[1024,768]{1,0:T(8,128)(2,1)} custom-call(s32[44]{0:T(128)} %fusion.74.order_ref, bf16[1024,1536]{1,0:T(8,128)(2,1)} %copy-done.79, bf16[4,1024,128]{2,1,0:T(8,128)(2,1)} %pad_maximum_fusion.17.bc_ref, f32[1024,8]{1,0:T(8,128)} %copy.99.marks_ref, f32[8,1024]{1,0:T(8,128)} %broadcast_in_dim.13.seg_row_ref, ...), custom_call_target="tpu_custom_call" | custom-call | flops 22548578304 | bytes 5877936 | tf_op jit(solution)/shard_map/pallas_call | solution.py:667
  164.5 8.7 %multiply_reduce_fusion.1 = (f32[1024]{0:T(1024)S(1)}, f32[1024,768]{1,0:T(8,128)}) fusion(bf16[1024,768]{1,0:T(8,128)(2,1)S(1)} %copy-done.21, bf16[2048,768]{1,0:T(8,128)(2,1)} %bitcast.397, bf16[1024,2048]{1,0:T(8,128)(2,1)} %copy-done.25, f32[2048]{0:T(1024)S(1)} %bitcast.364, f32[1024]{0:T(1024)S(1)} %copy-done.87), kind=kOutput, calls=%fused_computation.42 | convolution fusion | flops 3235904512 | bytes 12075008 | tf_op jit(solution)/shard_map/dot_general | solution.py:28
  179.4 4.2 multiply_convert_fusion.1
  196.5 19.8 %collective-permute-done.14 = bf16[256,2048]{1,0:T(8,128)(2,1)S(1)} collective-permute-done((bf16[256,2048]{1,0:T(8,128)(2,1)S(1)}, bf16[256,2048]{1,0:T(8,128)(2,1)S(1)}, u32[]{:S(2)}, u32[]{:S(2)}) %collective-permute-start.14) | collective-permute-done | bytes 1048608 | tf_op jit(solution)/shard_map/ppermute | solution.py:805
  220.6 10.9 %collective-permute-done.15 = bf16[128,2048]{1,0:T(8,128)(2,1)S(1)} collective-permute-done((bf16[128,2048]{1,0:T(8,128)(2,1)S(1)}, bf16[128,2048]{1,0:T(8,128)(2,1)S(1)}, u32[]{:S(2)}, u32[]{:S(2)}) %collective-permute-start.15) | collective-permute-done | bytes 524320 | tf_op jit(solution)/shard_map/ppermute | solution.py:805
  236.6 11.4 %collective-permute-done.18 = bf16[128,2048]{1,0:T(8,128)(2,1)} collective-permute-done((bf16[128,2048]{1,0:T(8,128)(2,1)}, bf16[128,2048]{1,0:T(8,128)(2,1)}, u32[]{:S(2)}, u32[]{:S(2)}) %collective-permute-start.18) | collective-permute-done | bytes 524320 | tf_op jit(solution)/shard_map/ppermute | solution.py:805
  255.5 11.5 %collective-permute-done.20 = bf16[128,2048]{1,0:T(8,128)(2,1)S(1)} collective-permute-done((bf16[128,2048]{1,0:T(8,128)(2,1)S(1)}, bf16[128,2048]{1,0:T(8,128)(2,1)S(1)}, u32[]{:S(2)}, u32[]{:S(2)}) %collective-permute-start.20) | collective-permute-done | bytes 524320 | tf_op jit(solution)/shard_map/ppermute | solution.py:805
  270.3 15.3 %collective-permute-done.19 = bf16[256,2048]{1,0:T(8,128)(2,1)S(1)} collective-permute-done((bf16[256,2048]{1,0:T(8,128)(2,1)S(1)}, bf16[256,2048]{1,0:T(8,128)(2,1)S(1)}, u32[]{:S(2)}, u32[]{:S(2)}) %collective-permute-start.19) | collective-permute-done | bytes 1048608 | tf_op jit(solution)/shard_map/ppermute | solution.py:805
  287.2 5.4 fusion.13
  292.9 5.8 multiply_convert_fusion.7
  302.4 3.8 multiply_convert_fusion.6
  309.2 6.3 convolution_convert_fusion.3
  317.4 3.2 constant_dynamic-update-slice_fusion.11
  320.6 7.1 %multiply_convert_fusion.5 = (bf16[512,1024]{1,0:T(8,128)(2,1)S(1)}, bf16[512,1024]{1,0:T(8,128)(2,1)S(1)}) fusion(f32[512,1024]{1,0:T(8,128)} %get-tuple-element.460, f32[512,1024]{1,0:T(8,128)} %copy-done.100, bf16[512,2048]{1,0:T(8,128)(2,1)} %pad_maximum_fusion.5, bf16[1024,2048]{1,0:T(8,128)(2,1)} %all-gather.13.cloned.1.call-done), kind=kOutput, calls=%fused_computation.81 | convolution fusion | flops 2153775104 | bytes 12582912 | tf_op jit(solution)/shard_map/dot_general | solution.py:38
  327.9 6.2 convolution_convert_fusion.6
  341.0 11.3 %convolution_convert_fusion = bf16[2048,2048]{1,0:T(8,128)(2,1)} fusion(bf16[1024,2048]{1,0:T(8,128)(2,1)S(1)} %copy-done.78, bf16[1024,2048]{1,0:T(8,128)(2,1)S(1)} %pad_maximum_fusion.2), kind=kOutput, calls=%fused_computation.6 | convolution fusion | flops 8594128896 | bytes 16777216 | tf_op jit(solution)/shard_map/dot_general | solution.py:32
  356.1 7.2 %fusion.107 = f32[512,2048]{1,0:T(8,128)S(1)} fusion(bf16[512,2048]{1,0:T(8,128)(2,1)S(1)} %copy-done.20, bf16[2048,2048]{1,0:T(8,128)(2,1)} %bitcast.390), kind=kOutput, calls=%fused_computation.357 | convolution fusion | flops 4294967296 | bytes 14680064 | tf_op jit(solution)/shard_map/dot_general | solution.py:38
  363.3 13.3 %collective-permute-done.22 = bf16[256,2048]{1,0:T(8,128)(2,1)S(1)} collective-permute-done((bf16[256,2048]{1,0:T(8,128)(2,1)S(1)}, bf16[256,2048]{1,0:T(8,128)(2,1)S(1)}, u32[]{:S(2)}, u32[]{:S(2)}) %collective-permute-start.22) | collective-permute-done | bytes 1048608 | tf_op jit(solution)/shard_map/ppermute | solution.py:805
  380.6 7.1 %collective-permute-done.23 = bf16[128,2048]{1,0:T(8,128)(2,1)S(1)} collective-permute-done((bf16[128,2048]{1,0:T(8,128)(2,1)S(1)}, bf16[128,2048]{1,0:T(8,128)(2,1)S(1)}, u32[]{:S(2)}, u32[]{:S(2)}) %collective-permute-start.23) | collective-permute-done | bytes 524320 | tf_op jit(solution)/shard_map/ppermute | solution.py:805
  396.8 4.4 fusion.32
  401.2 5.3 collective-permute-done.26
  411.3 3.7 convolution_convert_fusion.5
  415.1 12.0 %collective-permute-done.28 = bf16[256,2048]{1,0:T(8,128)(2,1)S(1)} collective-permute-done((bf16[256,2048]{1,0:T(8,128)(2,1)S(1)}, bf16[256,2048]{1,0:T(8,128)(2,1)S(1)}, u32[]{:S(2)}, u32[]{:S(2)}) %collective-permute-start.28) | collective-permute-done | bytes 1048608 | tf_op jit(solution)/shard_map/ppermute | solution.py:805
  430.6 5.6 multiply_reduce_fusion
  440.9 4.1 convolution_convert_fusion.4
  449.6 4.3 convolution_convert_fusion.8.grad_ref
  453.9 10.2 %shard_map.367 = bf16[1024,512]{1,0:T(8,128)(2,1)} custom-call(s32[44]{0:T(128)} %fusion.74.order_ref, bf16[1024,1536]{1,0:T(8,128)(2,1)} %copy-done.79, bf16[1024,256]{1,0:T(8,128)(2,1)} %convolution_convert_fusion.8.grad_ref, f32[1024,128]{1,0:T(8,128)} %get-tuple-element.112.cos_ref, f32[1024,128]{1,0:T(8,128)} %get-tuple-element.113.sin_ref, ...), custom_call_target="tpu_custom_call" | custom-call | flops 11811160064 | bytes 5865648 | tf_op jit(solution)/shard_map/pallas_call | solution.py:667
  464.1 4.8 fusion.16
  471.7 7.8 %convolution_convert_fusion.1 = bf16[2048,1280]{1,0:T(8,128)(2,1)} fusion(bf16[1024,1280]{1,0:T(8,128)(2,1)S(1)} %pad_maximum_fusion.3, bf16[1024,2048]{1,0:T(8,128)(2,1)S(1)} %copy-done.26, f32[2048]{0:T(1024)S(1)} %bitcast.365, f32[1024]{0:T(1024)S(1)} %copy-done.88), kind=kOutput, calls=%fused_computation.7 | convolution fusion | flops 5379719168 | bytes 12070912 | tf_op jit(solution)/shard_map/dot_general | solution.py:32
  483.0 41.4 %shard_map.368 = (bf16[1024,768]{1,0:T(8,128)(2,1)}, bf16[1024,128]{1,0:T(8,128)(2,1)}, bf16[4,1024,128]{2,1,0:T(8,128)(2,1)}, f32[8,768]{1,0:T(8,128)}, f32[8,512]{1,0:T(8,128)}, /*index=5*/f32[8,128]{1,0:T(8,128)}) custom-call(s32[44]{0:T(128)} %fusion.74.order_ref, bf16[1024,1536]{1,0:T(8,128)(2,1)} %copy-done.79, ...), custom_call_target="tpu_custom_call" | custom-call | flops 48318382080 | bytes 8806576 | tf_op jit(solution)/shard_map/pallas_call | solution.py:667
  535.8 3.5 all-to-all-start.2
  539.6 5.8 collective-permute-done.36
  556.7 10.1 %add_convert_fusion = bf16[2048,1024]{1,0:T(8,128)(2,1)} fusion(f32[2048,11]{1,0:T(8,128)} %reshape.358, bf16[1024,1024]{1,0:T(8,128)(2,1)} %pad_maximum_fusion.13, bf16[1024,2048]{1,0:T(8,128)(2,1)} %copy-done.25, f32[2048]{0:T(1024)S(1)} %bitcast.366, f32[1024]{0:T(1024)S(1)} %copy-done.88), kind=kOutput, calls=%fused_computation.5 | convolution fusion | flops 4307550208 | bytes 10588160 | tf_op jit(solution)/shard_map/dot_general | solution.py:32
  576.7 4.3 fusion.3
  581.1 5.9 fusion.34
  587.0 3.5 all-to-all-start.3
  590.5 7.6 %add_add_fusion = f32[512,2048]{1,0:T(8,128)} fusion(f32[512,2048]{1,0:T(8,128)} %fusion.3, f32[512,2048]{1,0:T(8,128)} %fusion.34, bf16[2048,1536]{1,0:T(8,128)(2,1)} %bitcast.335, bf16[1024,512]{1,0:T(8,128)(2,1)} %shard_map.367), kind=kOutput, calls=%fused_computation.11 | convolution fusion | flops 1075838976 | bytes 15204352 | tf_op jit(solution)/shard_map/dot_general | solution.py:38
  600.5 3.5 convert_add_fusion.2
  619.7 3.5 fusion.22
  623.2 5.3 reduce-scatter.14.cloned.1.call-done
  628.5 3.6 all-to-all-start.4
  632.9 5.9 all-to-all-done.4
  (566 shorter events, 205.6 us)
Async XLA Ops:
  7.2 95.1 %all-gather.7.cloned.1.call-start = ((), (), s32[]{:S(2)}) async-start(), calls=%async_computation.10 | async-start | bytes 7077888 | tf_op jit(solution)/shard_map/all_gather | solution.py:937
  31.8 132.5 %all-gather.9.cloned.1.call-start = ((), (), s32[]{:S(2)}) async-start(), calls=%async_computation.11 | async-start | bytes 3538944 | tf_op jit(solution)/shard_map/all_gather | solution.py:937
  32.0 12.2 %collective-permute-start = (bf16[128,2048]{1,0:T(8,128)(2,1)S(1)}, bf16[128,2048]{1,0:T(8,128)(2,1)S(1)}, u32[]{:S(2)}, u32[]{:S(2)}) collective-permute-start(bf16[128,2048]{1,0:T(8,128)(2,1)S(1)} %get-tuple-element.318), channel_id=1, source_target_pairs={{0,8},{8,0},{16,24},{24,16},{1,9},{9,1},{17,25},{25,17},{2,10},{10... | collective-permute-start | bytes 1572872 | tf_op jit(solution)/shard_map/ppermute | solution.py:805
  33.0 13.0 %collective-permute-start.1 = (bf16[128,2048]{1,0:T(8,128)(2,1)S(1)}, bf16[128,2048]{1,0:T(8,128)(2,1)S(1)}, u32[]{:S(2)}, u32[]{:S(2)}) collective-permute-start(bf16[128,2048]{1,0:T(8,128)(2,1)S(1)} %get-tuple-element.316), channel_id=1, source_target_pairs={{0,16},{8,24},{16,0},{24,8},{1,17},{9,25},{17,1},{25,9},{2,18},{10... | collective-permute-start | bytes 1572872 | tf_op jit(solution)/shard_map/ppermute | solution.py:805
  44.3 23.3 %collective-permute-start.2 = (bf16[256,2048]{1,0:T(8,128)(2,1)S(1)}, bf16[256,2048]{1,0:T(8,128)(2,1)S(1)}, u32[]{:S(2)}, u32[]{:S(2)}) collective-permute-start(bf16[256,2048]{1,0:T(8,128)(2,1)S(1)} %pad_maximum_fusion.15), channel_id=1, source_target_pairs={{0,16},{8,24},{16,0},{24,8},{1,17},{9,25},{17,1},{25,9},{2,18},{10... | collective-permute-start | bytes 3145736 | tf_op jit(solution)/shard_map/ppermute | solution.py:805
  46.1 22.2 %collective-permute-start.3 = (bf16[256,2048]{1,0:T(8,128)(2,1)S(1)}, bf16[256,2048]{1,0:T(8,128)(2,1)S(1)}, u32[]{:S(2)}, u32[]{:S(2)}) collective-permute-start(bf16[256,2048]{1,0:T(8,128)(2,1)S(1)} %pad_maximum_fusion.16), channel_id=1, source_target_pairs={{0,8},{8,0},{16,24},{24,16},{1,9},{9,1},{17,25},{25,17},{2,10},{10... | collective-permute-start | bytes 3145736 | tf_op jit(solution)/shard_map/ppermute | solution.py:805
  89.7 94.1 %all-gather.15.cloned.1.call-start = ((), (), s32[]{:S(2)}) async-start(), calls=%async_computation.19 | async-start | bytes 4718592 | tf_op jit(solution)/shard_map/all_gather | solution.py:1089
  90.7 196.5 %all-gather.11.cloned.1.call-start = ((), (), s32[]{:S(2)}) async-start(), calls=%async_computation.12 | async-start | bytes 9437184 | tf_op jit(solution)/shard_map/all_gather | solution.py:937
  102.0 218.6 %all-gather.13.cloned.1.call-start = ((), (), s32[]{:S(2)}) async-start(), calls=%async_computation.13 | async-start | bytes 4718592 | tf_op jit(solution)/shard_map/all_gather | solution.py:1112
  115.6 20.8 %collective-permute-start.4 = (bf16[1024,128]{1,0:T(8,128)(2,1)}, bf16[1024,128]{1,0:T(8,128)(2,1)}, u32[]{:S(2)}, u32[]{:S(2)}) collective-permute-start(bf16[1024,128]{1,0:T(8,128)(2,1)} %get-tuple-element.291), channel_id=1, source_target_pairs={{0,8},{8,0},{16,24},{24,16},{1,9},{9,1},{17,25},{25,17},{2,10},{10... | collective-permute-start | bytes 786440 | tf_op jit(solution)/shard_map/ppermute | solution.py:805
  116.7 19.7 %collective-permute-start.5 = (bf16[1024,128]{1,0:T(8,128)(2,1)}, bf16[1024,128]{1,0:T(8,128)(2,1)}, u32[]{:S(2)}, u32[]{:S(2)}) collective-permute-start(bf16[1024,128]{1,0:T(8,128)(2,1)} %get-tuple-element.291), channel_id=1, source_target_pairs={{0,16},{8,24},{16,0},{24,8},{1,17},{9,25},{17,1},{25,9},{2,18},{10... | collective-permute-start | bytes 786440 | tf_op jit(solution)/shard_map/ppermute | solution.py:805
  117.0 19.4 %collective-permute-start.6 = (bf16[1024,128]{1,0:T(8,128)(2,1)}, bf16[1024,128]{1,0:T(8,128)(2,1)}, u32[]{:S(2)}, u32[]{:S(2)}) collective-permute-start(bf16[1024,128]{1,0:T(8,128)(2,1)} %get-tuple-element.291), channel_id=1, source_target_pairs={{0,24},{8,16},{16,8},{24,0},{1,25},{9,17},{17,9},{25,1},{2,26},{10... | collective-permute-start | bytes 786440 | tf_op jit(solution)/shard_map/ppermute | solution.py:805
  119.2 19.4 %collective-permute-start.8 = (bf16[128,2048]{1,0:T(8,128)(2,1)S(1)}, bf16[128,2048]{1,0:T(8,128)(2,1)S(1)}, u32[]{:S(2)}, u32[]{:S(2)}) collective-permute-start(bf16[128,2048]{1,0:T(8,128)(2,1)S(1)} %get-tuple-element.314), channel_id=1, source_target_pairs={{0,16},{8,24},{16,0},{24,8},{1,17},{9,25},{17,1},{25,9},{2,18},{10... | collective-permute-start | bytes 1572872 | tf_op jit(solution)/shard_map/ppermute | solution.py:805
  120.3 18.4 %collective-permute-start.7 = (bf16[128,2048]{1,0:T(8,128)(2,1)S(1)}, bf16[128,2048]{1,0:T(8,128)(2,1)S(1)}, u32[]{:S(2)}, u32[]{:S(2)}) collective-permute-start(bf16[128,2048]{1,0:T(8,128)(2,1)S(1)} %get-tuple-element.315), channel_id=1, source_target_pairs={{0,8},{8,0},{16,24},{24,16},{1,9},{9,1},{17,25},{25,17},{2,10},{10... | collective-permute-start | bytes 1572872 | tf_op jit(solution)/shard_map/ppermute | solution.py:805
  138.8 23.8 %collective-permute-start.10 = (bf16[256,2048]{1,0:T(8,128)(2,1)S(1)}, bf16[256,2048]{1,0:T(8,128)(2,1)S(1)}, u32[]{:S(2)}, u32[]{:S(2)}) collective-permute-start(bf16[256,2048]{1,0:T(8,128)(2,1)S(1)} %pad_maximum_fusion.19), channel_id=1, source_target_pairs={{0,8},{8,0},{16,24},{24,16},{1,9},{9,1},{17,25},{25,17},{2,10},{10... | collective-permute-start | bytes 3145736 | tf_op jit(solution)/shard_map/ppermute | solution.py:805
  140.6 22.0 %collective-permute-start.9 = (bf16[256,2048]{1,0:T(8,128)(2,1)S(1)}, bf16[256,2048]{1,0:T(8,128)(2,1)S(1)}, u32[]{:S(2)}, u32[]{:S(2)}) collective-permute-start(bf16[256,2048]{1,0:T(8,128)(2,1)S(1)} %pad_maximum_fusion.18), channel_id=1, source_target_pairs={{0,16},{8,24},{16,0},{24,8},{1,17},{9,25},{17,1},{25,9},{2,18},{10... | collective-permute-start | bytes 3145736 | tf_op jit(solution)/shard_map/ppermute | solution.py:805
  191.0 25.4 %collective-permute-start.14 = (bf16[256,2048]{1,0:T(8,128)(2,1)S(1)}, bf16[256,2048]{1,0:T(8,128)(2,1)S(1)}, u32[]{:S(2)}, u32[]{:S(2)}) collective-permute-start(bf16[256,2048]{1,0:T(8,128)(2,1)S(1)} %get-tuple-element.298), channel_id=1, source_target_pairs={{0,16},{8,24},{16,0},{24,8},{1,17},{9,25},{17,1},{25,9},{2,18},{10... | collective-permute-start | bytes 3145736 | tf_op jit(solution)/shard_map/ppermute | solution.py:805
  192.4 25.0 %collective-permute-start.16 = (bf16[256,2048]{1,0:T(8,128)(2,1)S(1)}, bf16[256,2048]{1,0:T(8,128)(2,1)S(1)}, u32[]{:S(2)}, u32[]{:S(2)}) collective-permute-start(bf16[256,2048]{1,0:T(8,128)(2,1)S(1)} %get-tuple-element.299), channel_id=1, source_target_pairs={{0,8},{8,0},{16,24},{24,16},{1,9},{9,1},{17,25},{25,17},{2,10},{10... | collective-permute-start | bytes 3145736 | tf_op jit(solution)/shard_map/ppermute | solution.py:805
  218.4 13.1 %collective-permute-start.15 = (bf16[128,2048]{1,0:T(8,128)(2,1)S(1)}, bf16[128,2048]{1,0:T(8,128)(2,1)S(1)}, u32[]{:S(2)}, u32[]{:S(2)}) collective-permute-start(bf16[128,2048]{1,0:T(8,128)(2,1)S(1)} %slice.1521), channel_id=1, source_target_pairs={{0,8},{8,0},{16,24},{24,16},{1,9},{9,1},{17,25},{25,17},{2,10},{10... | collective-permute-start | bytes 1572872 | tf_op jit(solution)/shard_map/ppermute | solution.py:805
  220.0 12.8 %collective-permute-start.17 = (bf16[128,2048]{1,0:T(8,128)(2,1)S(1)}, bf16[128,2048]{1,0:T(8,128)(2,1)S(1)}, u32[]{:S(2)}, u32[]{:S(2)}) collective-permute-start(bf16[128,2048]{1,0:T(8,128)(2,1)S(1)} %slice.1520), channel_id=1, source_target_pairs={{0,16},{8,24},{16,0},{24,8},{1,17},{9,25},{17,1},{25,9},{2,18},{10... | collective-permute-start | bytes 1572872 | tf_op jit(solution)/shard_map/ppermute | solution.py:805
  235.8 12.3 %collective-permute-start.18 = (bf16[128,2048]{1,0:T(8,128)(2,1)}, bf16[128,2048]{1,0:T(8,128)(2,1)}, u32[]{:S(2)}, u32[]{:S(2)}) collective-permute-start(bf16[128,2048]{1,0:T(8,128)(2,1)} %get-tuple-element.310), channel_id=1, source_target_pairs={{0,8},{8,0},{16,24},{24,16},{1,9},{9,1},{17,25},{25,17},{2,10},{10... | collective-permute-start | bytes 1572872 | tf_op jit(solution)/shard_map/ppermute | solution.py:805
  236.4 154.0 %reduce-scatter.6.cloned.1.call-start = ((), (), s32[]{:S(2)}) async-start(), calls=%async_computation.14 | async-start | bytes 4718592 | tf_op jit(solution)/shard_map/reduce_scatter | solution.py:1167
  252.1 14.9 %collective-permute-start.20 = (bf16[128,2048]{1,0:T(8,128)(2,1)S(1)}, bf16[128,2048]{1,0:T(8,128)(2,1)S(1)}, u32[]{:S(2)}, u32[]{:S(2)}) collective-permute-start(bf16[128,2048]{1,0:T(8,128)(2,1)S(1)} %get-tuple-element.308), channel_id=1, source_target_pairs={{0,16},{8,24},{16,0},{24,8},{1,17},{9,25},{17,1},{25,9},{2,18},{10... | collective-permute-start | bytes 1572872 | tf_op jit(solution)/shard_map/ppermute | solution.py:805
  254.1 31.5 %collective-permute-start.19 = (bf16[256,2048]{1,0:T(8,128)(2,1)S(1)}, bf16[256,2048]{1,0:T(8,128)(2,1)S(1)}, u32[]{:S(2)}, u32[]{:S(2)}) collective-permute-start(bf16[256,2048]{1,0:T(8,128)(2,1)S(1)} %pad_maximum_fusion.20), channel_id=1, source_target_pairs={{0,16},{8,24},{16,0},{24,8},{1,17},{9,25},{17,1},{25,9},{2,18},{10... | collective-permute-start | bytes 3145736 | tf_op jit(solution)/shard_map/ppermute | solution.py:805
  267.1 18.5 %collective-permute-start.21 = (bf16[256,2048]{1,0:T(8,128)(2,1)S(1)}, bf16[256,2048]{1,0:T(8,128)(2,1)S(1)}, u32[]{:S(2)}, u32[]{:S(2)}) collective-permute-start(bf16[256,2048]{1,0:T(8,128)(2,1)S(1)} %pad_maximum_fusion.21), channel_id=1, source_target_pairs={{0,8},{8,0},{16,24},{24,16},{1,9},{9,1},{17,25},{25,17},{2,10},{10... | collective-permute-start | bytes 3145736 | tf_op jit(solution)/shard_map/ppermute | solution.py:805
  315.5 164.0 %reduce-scatter.8.cloned.1.call-start = ((), (), s32[]{:S(2)}) async-start(), calls=%async_computation.15 | async-start | bytes 9437184 | tf_op jit(solution)/shard_map/reduce_scatter | solution.py:1178
  352.4 204.3 %reduce-scatter.10.cloned.1.call-start = ((), (), s32[]{:S(2)}) async-start(), calls=%async_computation.16 | async-start | bytes 4718592 | tf_op jit(solution)/shard_map/reduce_scatter | solution.py:1208
  354.4 22.2 %collective-permute-start.22 = (bf16[256,2048]{1,0:T(8,128)(2,1)S(1)}, bf16[256,2048]{1,0:T(8,128)(2,1)S(1)}, u32[]{:S(2)}, u32[]{:S(2)}) collective-permute-start(bf16[256,2048]{1,0:T(8,128)(2,1)S(1)} %get-tuple-element.296), channel_id=1, source_target_pairs={{0,16},{8,24},{16,0},{24,8},{1,17},{9,25},{17,1},{25,9},{2,18},{10... | collective-permute-start | bytes 3145736 | tf_op jit(solution)/shard_map/ppermute | solution.py:805
  355.5 21.9 %collective-permute-start.24 = (bf16[256,2048]{1,0:T(8,128)(2,1)S(1)}, bf16[256,2048]{1,0:T(8,128)(2,1)S(1)}, u32[]{:S(2)}, u32[]{:S(2)}) collective-permute-start(bf16[256,2048]{1,0:T(8,128)(2,1)S(1)} %get-tuple-element.297), channel_id=1, source_target_pairs={{0,8},{8,0},{16,24},{24,16},{1,9},{9,1},{17,25},{25,17},{2,10},{10... | collective-permute-start | bytes 3145736 | tf_op jit(solution)/shard_map/ppermute | solution.py:805
  394.2 12.3 %collective-permute-start.26 = (bf16[128,2048]{1,0:T(8,128)(2,1)S(1)}, bf16[128,2048]{1,0:T(8,128)(2,1)S(1)}, u32[]{:S(2)}, u32[]{:S(2)}) collective-permute-start(bf16[128,2048]{1,0:T(8,128)(2,1)S(1)} %get-tuple-element.313), channel_id=1, source_target_pairs={{0,8},{8,0},{16,24},{24,16},{1,9},{9,1},{17,25},{25,17},{2,10},{10... | collective-permute-start | bytes 1572872 | tf_op jit(solution)/shard_map/ppermute | solution.py:805
  395.4 14.7 %collective-permute-start.27 = (bf16[128,2048]{1,0:T(8,128)(2,1)S(1)}, bf16[128,2048]{1,0:T(8,128)(2,1)S(1)}, u32[]{:S(2)}, u32[]{:S(2)}) collective-permute-start(bf16[128,2048]{1,0:T(8,128)(2,1)S(1)} %get-tuple-element.311), channel_id=1, source_target_pairs={{0,16},{8,24},{16,0},{24,8},{1,17},{9,25},{17,1},{25,9},{2,18},{10... | collective-permute-start | bytes 1572872 | tf_op jit(solution)/shard_map/ppermute | solution.py:805
  406.6 20.5 %collective-permute-start.28 = (bf16[256,2048]{1,0:T(8,128)(2,1)S(1)}, bf16[256,2048]{1,0:T(8,128)(2,1)S(1)}, u32[]{:S(2)}, u32[]{:S(2)}) collective-permute-start(bf16[256,2048]{1,0:T(8,128)(2,1)S(1)} %pad_maximum_fusion.22), channel_id=1, source_target_pairs={{0,16},{8,24},{16,0},{24,8},{1,17},{9,25},{17,1},{25,9},{2,18},{10... | collective-permute-start | bytes 3145736 | tf_op jit(solution)/shard_map/ppermute | solution.py:805
  410.2 16.9 %collective-permute-start.29 = (bf16[256,2048]{1,0:T(8,128)(2,1)S(1)}, bf16[256,2048]{1,0:T(8,128)(2,1)S(1)}, u32[]{:S(2)}, u32[]{:S(2)}) collective-permute-start(bf16[256,2048]{1,0:T(8,128)(2,1)S(1)} %pad_maximum_fusion.23), channel_id=1, source_target_pairs={{0,8},{8,0},{16,24},{24,16},{1,9},{9,1},{17,25},{25,17},{2,10},{10... | collective-permute-start | bytes 3145736 | tf_op jit(solution)/shard_map/ppermute | solution.py:805
  436.1 11.4 %collective-permute-start.30 = (f32[1024]{0:T(1024)S(1)}, f32[1024]{0:T(1024)S(1)}, u32[]{:S(2)}, u32[]{:S(2)}) collective-permute-start(f32[1024]{0:T(1024)S(1)} %get-tuple-element.461), channel_id=1, source_target_pairs={{0,8},{8,0},{16,24},{24,16},{1,9},{9,1},{17,25},{25,17},{2,10},{10... | collective-permute-start | bytes 12296 | tf_op jit(solution)/shard_map/ppermute | solution.py:805
  447.7 139.3 %reduce-scatter.12.cloned.1.call-start = ((), (), s32[]{:S(2)}) async-start(), calls=%async_computation.17 | async-start | bytes 5898240 | tf_op jit(solution)/shard_map/reduce_scatter | solution.py:1220
  481.0 44.9 %collective-permute-start.33 = (bf16[256,2048]{1,0:T(8,128)(2,1)}, bf16[256,2048]{1,0:T(8,128)(2,1)S(1)}, u32[]{:S(2)}, u32[]{:S(2)}) collective-permute-start(bf16[256,2048]{1,0:T(8,128)(2,1)} %get-tuple-element.295), channel_id=1, source_target_pairs={{0,16},{8,24},{16,0},{24,8},{1,17},{9,25},{17,1},{25,9},{2,18},{10... | collective-permute-start | bytes 3145736 | tf_op jit(solution)/shard_map/ppermute | solution.py:805
  482.4 43.5 %collective-permute-start.34 = (bf16[256,2048]{1,0:T(8,128)(2,1)}, bf16[256,2048]{1,0:T(8,128)(2,1)S(1)}, u32[]{:S(2)}, u32[]{:S(2)}) collective-permute-start(bf16[256,2048]{1,0:T(8,128)(2,1)} %get-tuple-element.294), channel_id=1, source_target_pairs={{0,8},{8,0},{16,24},{24,16},{1,9},{9,1},{17,25},{25,17},{2,10},{10... | collective-permute-start | bytes 3145736 | tf_op jit(solution)/shard_map/ppermute | solution.py:805
  528.5 11.0 %collective-permute-start.35 = (bf16[1024,128]{1,0:T(8,128)(2,1)}, bf16[1024,128]{1,0:T(8,128)(2,1)S(1)}, u32[]{:S(2)}, u32[]{:S(2)}) collective-permute-start(bf16[1024,128]{1,0:T(8,128)(2,1)} %get-tuple-element.304), channel_id=1, source_target_pairs={{0,8},{8,0},{16,24},{24,16},{1,9},{9,1},{17,25},{25,17},{2,10},{10... | collective-permute-start | bytes 786440 | tf_op jit(solution)/shard_map/ppermute | solution.py:805
  529.9 15.5 %collective-permute-start.36 = (bf16[1024,128]{1,0:T(8,128)(2,1)}, bf16[1024,128]{1,0:T(8,128)(2,1)S(1)}, u32[]{:S(2)}, u32[]{:S(2)}) collective-permute-start(bf16[1024,128]{1,0:T(8,128)(2,1)} %get-tuple-element.306), channel_id=1, source_target_pairs={{0,16},{8,24},{16,0},{24,8},{1,17},{9,25},{17,1},{25,9},{2,18},{10... | collective-permute-start | bytes 786440 | tf_op jit(solution)/shard_map/ppermute | solution.py:805
  530.6 14.7 %collective-permute-start.37 = (bf16[1024,128]{1,0:T(8,128)(2,1)}, bf16[1024,128]{1,0:T(8,128)(2,1)}, u32[]{:S(2)}, u32[]{:S(2)}) collective-permute-start(bf16[1024,128]{1,0:T(8,128)(2,1)} %get-tuple-element.305), channel_id=1, source_target_pairs={{0,24},{8,16},{16,8},{24,0},{1,25},{9,17},{17,9},{25,1},{2,26},{10... | collective-permute-start | bytes 786440 | tf_op jit(solution)/shard_map/ppermute | solution.py:805
  535.8 20.9 %all-to-all-start.2 = ((bf16[4,64,2048]{2,1,0:T(8,128)(2,1)}), bf16[4,64,2048]{2,1,0:T(8,128)(2,1)S(1)}, u32[]{:S(2)}, u32[]{:S(2)}) async-start(bf16[4,64,2048]{2,1,0:T(8,128)(2,1)} %reduce-scatter.8.cloned.1.call-done), calls=%async_computation.5 | async-start | bytes 2097152 | tf_op jit(solution)/shard_map/all_to_all | solution.py:946
  539.3 89.2 %reduce-scatter.14.cloned.1.call-start = ((), (), s32[]{:S(2)}) async-start(), calls=%async_computation.18 | async-start | bytes 4718592 | tf_op jit(solution)/shard_map/reduce_scatter | solution.py:1268
  553.7 13.2 %collective-permute-start.38 = (bf16[128,2048]{1,0:T(8,128)(2,1)}, bf16[128,2048]{1,0:T(8,128)(2,1)S(1)}, u32[]{:S(2)}, u32[]{:S(2)}) collective-permute-start(bf16[128,2048]{1,0:T(8,128)(2,1)} %slice.1517), channel_id=1, source_target_pairs={{0,8},{8,0},{16,24},{24,16},{1,9},{9,1},{17,25},{25,17},{2,10},{10... | collective-permute-start | bytes 1572872 | tf_op jit(solution)/shard_map/ppermute | solution.py:805
  553.7 13.2 %collective-permute-start.39 = (bf16[128,2048]{1,0:T(8,128)(2,1)}, bf16[128,2048]{1,0:T(8,128)(2,1)}, u32[]{:S(2)}, u32[]{:S(2)}) collective-permute-start(bf16[128,2048]{1,0:T(8,128)(2,1)} %slice.1516), channel_id=1, source_target_pairs={{0,16},{8,24},{16,0},{24,8},{1,17},{9,25},{17,1},{25,9},{2,18},{10... | collective-permute-start | bytes 1572872 | tf_op jit(solution)/shard_map/ppermute | solution.py:805
  574.0 26.5 %collective-permute-start.40 = (bf16[256,2048]{1,0:T(8,128)(2,1)}, bf16[256,2048]{1,0:T(8,128)(2,1)}, u32[]{:S(2)}, u32[]{:S(2)}) collective-permute-start(bf16[256,2048]{1,0:T(8,128)(2,1)} %get-tuple-element.293), channel_id=1, source_target_pairs={{0,16},{8,24},{16,0},{24,8},{1,17},{9,25},{17,1},{25,9},{2,18},{10... | collective-permute-start | bytes 3145736 | tf_op jit(solution)/shard_map/ppermute | solution.py:805
  574.7 25.8 %collective-permute-start.41 = (bf16[256,2048]{1,0:T(8,128)(2,1)}, bf16[256,2048]{1,0:T(8,128)(2,1)}, u32[]{:S(2)}, u32[]{:S(2)}) collective-permute-start(bf16[256,2048]{1,0:T(8,128)(2,1)} %get-tuple-element.292), channel_id=1, source_target_pairs={{0,8},{8,0},{16,24},{24,16},{1,9},{9,1},{17,25},{25,17},{2,10},{10... | collective-permute-start | bytes 3145736 | tf_op jit(solution)/shard_map/ppermute | solution.py:805
  587.0 13.5 %all-to-all-start.3 = ((bf16[4,64,1280]{2,1,0:T(8,128)(2,1)}), bf16[4,64,1280]{2,1,0:T(8,128)(2,1)S(1)}, u32[]{:S(2)}, u32[]{:S(2)}) async-start(bf16[4,64,1280]{2,1,0:T(8,128)(2,1)} %reduce-scatter.12.cloned.1.call-done), calls=%async_computation.7 | async-start | bytes 1310720 | tf_op jit(solution)/shard_map/all_to_all | solution.py:946
  604.6 12.4 %collective-permute-start.42 = (bf16[128,2048]{1,0:T(8,128)(2,1)S(1)}, bf16[128,2048]{1,0:T(8,128)(2,1)S(1)}, u32[]{:S(2)}, u32[]{:S(2)}) collective-permute-start(bf16[128,2048]{1,0:T(8,128)(2,1)S(1)} %slice.1515), channel_id=1, source_target_pairs={{0,8},{8,0},{16,24},{24,16},{1,9},{9,1},{17,25},{25,17},{2,10},{10... | collective-permute-start | bytes 1572872 | tf_op jit(solution)/shard_map/ppermute | solution.py:805
  (114 other events, 1580.0 us)
Sparse Core Ops, SparseCore 0:
  31.9 64.4 all-gather.6
  98.5 36.9 all-gather.8
  137.7 46.0 all-gather.14
  185.9 80.7 all-gather.10
  268.1 45.6 all-gather.12
  316.0 48.7 reduce-scatter.5
  367.0 87.7 reduce-scatter.7
  457.1 48.3 reduce-scatter.9
  507.8 58.0 reduce-scatter.11
  581.2 47.2 reduce-scatter.13
where the time goes:
time: 658 us; the launch traced here: 651 us
  waiting for transfers between devices  167 us (25%)
  matrix products  147 us (22%)
  local copies, waits for them, and re-layouts  79.3 us (12%)
  Pallas kernels  78.7 us (12%)
  other arithmetic  68.5 us (10%)
  starting transfers between devices  59 us (9%)
  blocking collectives  34.7 us (5%)
  between operations  16.7 us (3%)
    ppermute x44, waiting for transfers between devices, swap_seq(): lax.ppermute(value, 'seq', [(place, place ^ bit) for place in range(count)])  153 us
    pallas_call x4, Pallas kernels, local_call(): pl.pallas_call(kernel, out_shape=outs, in_specs=[pl.BlockSpec(memory_spac...  78.7 us
    dot_general x12, matrix products, input_grad(): lax.dot_general(grad_rows, weights, (((1,), (1,)), ((), ())), preferred_e...  55.9 us
    dot_general x12, matrix products, mat_product(): return jnp.dot(left_op, right_op, preferred_element_type=jnp.float32)  50.2 us
    ppermute x44, starting transfers between devices, swap_seq(): lax.ppermute(value, 'seq', [(place, place ^ bit) for place in range(count)])  47.3 us
    dot_general x6, matrix products, weight_grad(): lax.dot_general(left_op, right_op, (((0,), (0,)), ((), ())), preferred_el...  40.9 us
    all_to_all x2, blocking collectives, columns_exchange(): lax.all_to_all(blocks, 'seq', split_axis=0, concat_axis=0, tiled=True)  34.7 us
    unnamed x226, local copies, waits for them, and re-layouts  28.5 us
  transfers between devices with their start and end apart: 57, of which 25 were waited for; matrix products, arithmetic and copies ran while one was open for 40% of the time, Pallas kernels for 12%

commit v1 on v0

--- a/solution.py
+++ b/solution.py
@@ -16,7 +16,7 @@
 STATE = 256
 BLOCK = 256
 LANES = 128
-KERNEL_VMEM = 56 * 1024 * 1024
+MIB = 1024 * 1024
 
 
 epsilon = 1e-05
@@ -661,7 +661,7 @@
     lax.fori_loop(0, blocks, last_block, jnp.zeros((1, LANES), jnp.float32))
 
 
-def local_call(kernel, outs, scratch, flops, operands):
+def local_call(kernel, outs, scratch, flops, vmem, operands):
     moved = sum(part.size * part.dtype.itemsize for part in operands)
     moved += sum(part.size * part.dtype.itemsize for part in outs)
     return pl.pallas_call(
@@ -671,7 +671,7 @@
         + [pl.BlockSpec(memory_space=pltpu.VMEM)] * (len(operands) - 1),
         out_specs=[pl.BlockSpec(memory_space=pltpu.VMEM)] * len(outs),
         scratch_shapes=scratch,
-        compiler_params=pltpu.CompilerParams(vmem_limit_bytes=KERNEL_VMEM),
+        compiler_params=pltpu.CompilerParams(vmem_limit_bytes=vmem * MIB),
         cost_estimate=pl.CostEstimate(flops=flops, bytes_accessed=moved, transcendentals=0),
     )(*operands)
 
@@ -692,6 +692,7 @@
             pltpu.VMEM((length, HEAD_DIM), low),
         ],
         36 * length * length * q_width,
+        22,
         (order, narrow, cosine, sine, marks, seg_row),
     )
 
@@ -711,6 +712,7 @@
             pltpu.VMEM((length, HEAD_DIM), jnp.float32),
         ],
         44 * length * length * q_width,
+        24,
         (order, narrow, grad, cosine, sine, marks, seg_row, lse),
     )[0]
 
@@ -743,6 +745,7 @@
             pltpu.VMEM((BLOCK, width), full),
         ],
         28 * length * length * width,
+        34,
         (order, narrow, bc, marks, seg_row, x_taps, bc_taps, heads),
     )[0]
 
@@ -776,6 +779,7 @@
             pltpu.VMEM((BLOCK, width + LANES + 2 * STATE), low),
         ],
         60 * length * length * width,
+        50,
         (order, narrow, bc, grad, marks, seg_row, x_taps, bc_taps, heads),
     )
 

time: 658 us -> 652 us (level)
  Pallas kernels: 78.7 us -> 69.3 us
    pallas_call x4, Pallas kernels: 78.7 us -> 69.3 us  [local_call(): pl.pallas_call(kernel, out_shape=outs, in_specs=[pl.BlockSpec(memory_spac...]
    unnamed x226 -> x254, local copies, waits for them, and re-layouts: 28.5 us -> 29.3 us
  transfers between devices with their start and end apart: 57 -> 57, of which waited for: 25 -> 28; matrix products, arithmetic and copies ran while one was open for 40% -> 40% of each run, Pallas kernels for 12% -> 11%
where the time goes in v1:
time: 652 us; the launch traced here: 646 us
  waiting for transfers between devices  173 us (27%)
  matrix products  147 us (23%)
  local copies, waits for them, and re-layouts  74.3 us (11%)
  Pallas kernels  69.3 us (11%)
  other arithmetic  68.5 us (11%)
  starting transfers between devices  62.2 us (10%)
  blocking collectives  34.7 us (5%)
  between operations  17 us (3%)
    ppermute x44, waiting for transfers between devices, swap_seq(): lax.ppermute(value, 'seq', [(place, place ^ bit) for place in range(count)])  159 us
    pallas_call x4, Pallas kernels, local_call(): pl.pallas_call(kernel, out_shape=outs, in_specs=[pl.BlockSpec(memory_spac...  69.3 us
    dot_general x12, matrix products, input_grad(): lax.dot_general(grad_rows, weights, (((1,), (1,)), ((), ())), preferred_e...  55.5 us
    dot_general x12, matrix products, mat_product(): return jnp.dot(left_op, right_op, preferred_element_type=jnp.float32)  50.4 us
    ppermute x44, starting transfers between devices, swap_seq(): lax.ppermute(value, 'seq', [(place, place ^ bit) for place in range(count)])  49.8 us
    dot_general x6, matrix products, weight_grad(): lax.dot_general(left_op, right_op, (((0,), (0,)), ((), ())), preferred_el...  41 us
    all_to_all x2, blocking collectives, columns_exchange(): lax.all_to_all(blocks, 'seq', split_axis=0, concat_axis=0, tiled=True)  34.7 us
    unnamed x254, local copies, waits for them, and re-layouts  29.3 us
  transfers between devices with their start and end apart: 57, of which 28 were waited for; matrix products, arithmetic and copies ran while one was open for 40% of the time, Pallas kernels for 11%

profile of v1, /device:TPU:0, one launch (start us, length us, event | category | flops | bytes accessed | tf_op | source)
XLA Modules:
  0.0 645.8 jit_solution(1125209579128196189)
XLA Ops:
  15.3 16.4 %all_to_all.25 = bf16[4,64,1536]{2,1,0:T(8,128)(2,1)} all-to-all(bf16[4,64,1536]{2,1,0:T(8,128)(2,1)S(1)} %pad_maximum_fusion.26), channel_id=1, replica_groups=mesh['seq'=4,'fsdp'=8] {'seq'}, dimensions={0} | all-to-all | bytes 1572864 | tf_op jit(solution)/shard_map/all_to_all | solution.py:937
  33.5 10.6 %collective-permute-done = bf16[128,2048]{1,0:T(8,128)(2,1)S(1)} collective-permute-done((bf16[128,2048]{1,0:T(8,128)(2,1)S(1)}, bf16[128,2048]{1,0:T(8,128)(2,1)S(1)}, u32[]{:S(2)}, u32[]{:S(2)}) %collective-permute-start) | collective-permute-done | bytes 524320 | tf_op jit(solution)/shard_map/ppermute | solution.py:809
  46.5 21.1 %collective-permute-done.2 = bf16[256,2048]{1,0:T(8,128)(2,1)S(1)} collective-permute-done((bf16[256,2048]{1,0:T(8,128)(2,1)S(1)}, bf16[256,2048]{1,0:T(8,128)(2,1)S(1)}, u32[]{:S(2)}, u32[]{:S(2)}) %collective-permute-start.2) | collective-permute-done | bytes 1048608 | tf_op jit(solution)/shard_map/ppermute | solution.py:809
  70.6 18.3 %all_to_all.26 = bf16[4,64,2816]{2,1,0:T(8,128)(2,1)S(1)} all-to-all(bf16[4,64,2816]{2,1,0:T(8,128)(2,1)S(1)} %pad_maximum_fusion.14), channel_id=1, replica_groups=mesh['seq'=4,'fsdp'=8] {'seq'}, dimensions={0} | all-to-all | bytes 2883584 | tf_op jit(solution)/shard_map/all_to_all | solution.py:937
  103.0 11.1 %convolution_convert_fusion.2.narrow_ref = bf16[1024,1536]{1,0:T(8,128)(2,1)S(1)} fusion(bf16[2048,1536]{1,0:T(8,128)(2,1)} %bitcast.334, bf16[1024,2048]{1,0:T(8,128)(2,1)} %copy-done.50, f32[2048]{0:T(1024)S(1)} %bitcast.363, f32[1024]{0:T(1024)S(1)} %add_rsqrt_fusion), kind=kOutput, calls=%fused_computation.16 | convolution fusion | flops 6452412416 | bytes 13643776 | tf_op jit(solution)/shard_map/dot_general | solution.py:28
  120.5 5.2 shard_map.365
  131.7 4.8 collective-permute-done.8
  141.0 16.3 %shard_map.366 = bf16[1024,768]{1,0:T(8,128)(2,1)S(1)} custom-call(s32[44]{0:T(128)S(1)} %fusion.74.order_ref, bf16[1024,1536]{1,0:T(8,128)(2,1)S(1)} %copy-done.13, bf16[4,1024,128]{2,1,0:T(8,128)(2,1)S(1)} %pad_maximum_fusion.17.bc_ref, f32[1024,8]{1,0:T(8,128)S(1)} %copy.99.marks_ref, f32[8,1024]{1,0:T(8,128)S(1)} %broadcast_in_dim.13.seg_row_ref, ...), custom_call_target="tpu_custom_call" | custom-call | flops 22548578304 | bytes 5877936 | tf_op jit(solution)/shard_map/pallas_call | solution.py:667
  162.8 8.8 %multiply_reduce_fusion.1 = (f32[1024]{0:T(1024)S(1)}, f32[1024,768]{1,0:T(8,128)}) fusion(bf16[1024,768]{1,0:T(8,128)(2,1)S(1)} %shard_map.366, bf16[2048,768]{1,0:T(8,128)(2,1)} %bitcast.397, bf16[1024,2048]{1,0:T(8,128)(2,1)} %copy-done.50, f32[2048]{0:T(1024)S(1)} %bitcast.364, f32[1024]{0:T(1024)S(1)} %add_rsqrt_fusion), kind=kOutput, calls=%fused_computation.42 | convolution fusion | flops 3235904512 | bytes 12075008 | tf_op jit(solution)/shard_map/dot_general | solution.py:28
  179.8 4.2 multiply_convert_fusion.1
  196.5 19.7 %collective-permute-done.14 = bf16[256,2048]{1,0:T(8,128)(2,1)S(1)} collective-permute-done((bf16[256,2048]{1,0:T(8,128)(2,1)S(1)}, bf16[256,2048]{1,0:T(8,128)(2,1)S(1)}, u32[]{:S(2)}, u32[]{:S(2)}) %collective-permute-start.14) | collective-permute-done | bytes 1048608 | tf_op jit(solution)/shard_map/ppermute | solution.py:809
  220.6 10.9 %collective-permute-done.15 = bf16[128,2048]{1,0:T(8,128)(2,1)S(1)} collective-permute-done((bf16[128,2048]{1,0:T(8,128)(2,1)S(1)}, bf16[128,2048]{1,0:T(8,128)(2,1)S(1)}, u32[]{:S(2)}, u32[]{:S(2)}) %collective-permute-start.15) | collective-permute-done | bytes 524320 | tf_op jit(solution)/shard_map/ppermute | solution.py:809
  236.1 11.4 %collective-permute-done.18 = bf16[128,2048]{1,0:T(8,128)(2,1)} collective-permute-done((bf16[128,2048]{1,0:T(8,128)(2,1)}, bf16[128,2048]{1,0:T(8,128)(2,1)}, u32[]{:S(2)}, u32[]{:S(2)}) %collective-permute-start.18) | collective-permute-done | bytes 524320 | tf_op jit(solution)/shard_map/ppermute | solution.py:809
  254.9 11.5 %collective-permute-done.20 = bf16[128,2048]{1,0:T(8,128)(2,1)S(1)} collective-permute-done((bf16[128,2048]{1,0:T(8,128)(2,1)S(1)}, bf16[128,2048]{1,0:T(8,128)(2,1)S(1)}, u32[]{:S(2)}, u32[]{:S(2)}) %collective-permute-start.20) | collective-permute-done | bytes 524320 | tf_op jit(solution)/shard_map/ppermute | solution.py:809
  269.9 15.1 %collective-permute-done.19 = bf16[256,2048]{1,0:T(8,128)(2,1)S(1)} collective-permute-done((bf16[256,2048]{1,0:T(8,128)(2,1)S(1)}, bf16[256,2048]{1,0:T(8,128)(2,1)S(1)}, u32[]{:S(2)}, u32[]{:S(2)}) %collective-permute-start.19) | collective-permute-done | bytes 1048608 | tf_op jit(solution)/shard_map/ppermute | solution.py:809
  286.6 5.4 fusion.13
  292.3 5.8 multiply_convert_fusion.7
  301.8 3.8 multiply_convert_fusion.6
  308.5 6.2 convolution_convert_fusion.3
  319.9 7.3 %multiply_convert_fusion.5 = (bf16[512,1024]{1,0:T(8,128)(2,1)S(1)}, bf16[512,1024]{1,0:T(8,128)(2,1)S(1)}) fusion(f32[512,1024]{1,0:T(8,128)} %get-tuple-element.460, f32[512,1024]{1,0:T(8,128)} %copy-done.114, bf16[512,2048]{1,0:T(8,128)(2,1)} %pad_maximum_fusion.5, bf16[1024,2048]{1,0:T(8,128)(2,1)} %all-gather.13.cloned.1.call-done), kind=kOutput, calls=%fused_computation.81 | convolution fusion | flops 2153775104 | bytes 12582912 | tf_op jit(solution)/shard_map/dot_general | solution.py:38
  327.4 6.2 convolution_convert_fusion.6
  340.6 11.4 %convolution_convert_fusion = bf16[2048,2048]{1,0:T(8,128)(2,1)} fusion(bf16[1024,2048]{1,0:T(8,128)(2,1)S(1)} %copy-done.95, bf16[1024,2048]{1,0:T(8,128)(2,1)S(1)} %pad_maximum_fusion.2), kind=kOutput, calls=%fused_computation.6 | convolution fusion | flops 8594128896 | bytes 16777216 | tf_op jit(solution)/shard_map/dot_general | solution.py:32
  355.8 7.2 %fusion.107 = f32[512,2048]{1,0:T(8,128)S(1)} fusion(bf16[512,2048]{1,0:T(8,128)(2,1)S(1)} %copy-done.46, bf16[2048,2048]{1,0:T(8,128)(2,1)} %bitcast.390), kind=kOutput, calls=%fused_computation.357 | convolution fusion | flops 4294967296 | bytes 14680064 | tf_op jit(solution)/shard_map/dot_general | solution.py:38
  363.0 12.2 %collective-permute-done.22 = bf16[256,2048]{1,0:T(8,128)(2,1)S(1)} collective-permute-done((bf16[256,2048]{1,0:T(8,128)(2,1)S(1)}, bf16[256,2048]{1,0:T(8,128)(2,1)S(1)}, u32[]{:S(2)}, u32[]{:S(2)}) %collective-permute-start.22) | collective-permute-done | bytes 1048608 | tf_op jit(solution)/shard_map/ppermute | solution.py:809
  380.6 6.8 %collective-permute-done.23 = bf16[128,2048]{1,0:T(8,128)(2,1)S(1)} collective-permute-done((bf16[128,2048]{1,0:T(8,128)(2,1)S(1)}, bf16[128,2048]{1,0:T(8,128)(2,1)S(1)}, u32[]{:S(2)}, u32[]{:S(2)}) %collective-permute-start.23) | collective-permute-done | bytes 524320 | tf_op jit(solution)/shard_map/ppermute | solution.py:809
  390.1 3.5 fusion.18
  397.2 4.4 fusion.32
  401.6 6.1 collective-permute-done.26
  411.9 3.7 convolution_convert_fusion.5
  415.7 11.7 %collective-permute-done.28 = bf16[256,2048]{1,0:T(8,128)(2,1)S(1)} collective-permute-done((bf16[256,2048]{1,0:T(8,128)(2,1)S(1)}, bf16[256,2048]{1,0:T(8,128)(2,1)S(1)}, u32[]{:S(2)}, u32[]{:S(2)}) %collective-permute-start.28) | collective-permute-done | bytes 1048608 | tf_op jit(solution)/shard_map/ppermute | solution.py:809
  430.4 5.6 multiply_reduce_fusion
  440.8 4.1 convolution_convert_fusion.4
  449.5 3.6 convolution_convert_fusion.8.grad_ref
  453.3 6.9 %shard_map.367 = bf16[1024,512]{1,0:T(8,128)(2,1)S(1)} custom-call(s32[44]{0:T(128)S(1)} %copy-done.20, bf16[1024,1536]{1,0:T(8,128)(2,1)S(1)} %copy-done.14, bf16[1024,256]{1,0:T(8,128)(2,1)S(1)} %convolution_convert_fusion.8.grad_ref, f32[1024,128]{1,0:T(8,128)S(1)} %copy-done.3, f32[1024,128]{1,0:T(8,128)S(1)} %copy-done.5, f32[1024,8]{1,0:T(8,128)S(1)} %copy-done.7, ...), custom_call_target="tpu_custom_call" | custom-call | flops 11811160064 | bytes 5865648 | tf_op jit(solution)/shard_map/pallas_call | solution.py:667
  466.2 7.8 %convolution_convert_fusion.1 = bf16[2048,1280]{1,0:T(8,128)(2,1)} fusion(bf16[1024,1280]{1,0:T(8,128)(2,1)S(1)} %pad_maximum_fusion.3, bf16[1024,2048]{1,0:T(8,128)(2,1)S(1)} %copy-done.51, f32[2048]{0:T(1024)S(1)} %bitcast.365, f32[1024]{0:T(1024)S(1)} %copy-done.103), kind=kOutput, calls=%fused_computation.7 | convolution fusion | flops 5379719168 | bytes 12070912 | tf_op jit(solution)/shard_map/dot_general | solution.py:32
  480.9 40.9 %shard_map.368 = (bf16[1024,768]{1,0:T(8,128)(2,1)}, bf16[1024,128]{1,0:T(8,128)(2,1)S(1)}, bf16[4,1024,128]{2,1,0:T(8,128)(2,1)S(1)}, f32[8,768]{1,0:T(8,128)S(...) custom-call(s32[44]{0:T(128)S(1)} %copy-done.20, bf16[1024,1536]{1,0:T(8,128)(2,1)} %copy-done.12, ...), custom_call_target="tpu_custom_call" | custom-call | flops 48318382080 | bytes 8806576 | tf_op jit(solution)/shard_map/pallas_call | solution.py:667
  532.5 4.2 all-to-all-start.2
  537.2 3.5 convert_add_fusion.4
  550.0 10.2 %add_convert_fusion = bf16[2048,1024]{1,0:T(8,128)(2,1)} fusion(f32[2048,11]{1,0:T(8,128)} %reshape.358, bf16[1024,1024]{1,0:T(8,128)(2,1)} %pad_maximum_fusion.13, bf16[1024,2048]{1,0:T(8,128)(2,1)} %copy-done.50, f32[2048]{0:T(1024)S(1)} %bitcast.366, f32[1024]{0:T(1024)S(1)} %copy-done.103), kind=kOutput, calls=%fused_computation.5 | convolution fusion | flops 4307550208 | bytes 10588160 | tf_op jit(solution)/shard_map/dot_general | solution.py:32
  570.7 4.3 fusion.3
  575.0 5.9 fusion.34
  580.9 3.5 all-to-all-start.3
  584.4 7.4 %add_add_fusion = f32[512,2048]{1,0:T(8,128)} fusion(f32[512,2048]{1,0:T(8,128)} %fusion.3, f32[512,2048]{1,0:T(8,128)} %fusion.34, bf16[2048,1536]{1,0:T(8,128)(2,1)} %bitcast.335, bf16[1024,512]{1,0:T(8,128)(2,1)S(1)} %shard_map.367), kind=kOutput, calls=%fused_computation.11 | convolution fusion | flops 1075838976 | bytes 15204352 | tf_op jit(solution)/shard_map/dot_general | solution.py:38
  592.5 3.5 convert_add_fusion.2
  612.7 3.5 fusion.22
  616.2 6.8 %reduce-scatter.14.cloned.1.call-done = bf16[4,64,1024]{2,1,0:T(8,128)(2,1)} async-done(((bf16[4,512,1024]{2,1,0:T(8,128)(2,1)}), bf16[4,64,1024]{2,1,0:T(8,128)(2,1)}) %reduce-scatter.14.cloned.1.call-update) | async-done | bytes 524304 | tf_op jit(solution)/shard_map/reduce_scatter | solution.py:1272
  623.0 3.7 all-to-all-start.4
  627.4 5.9 all-to-all-done.4
  (594 shorter events, 210.6 us)
Async XLA Ops:
  7.2 94.3 %all-gather.7.cloned.1.call-start = ((), (), s32[]{:S(2)}) async-start(), calls=%async_computation.10 | async-start | bytes 7077888 | tf_op jit(solution)/shard_map/all_gather | solution.py:941
  31.8 131.0 %all-gather.9.cloned.1.call-start = ((), (), s32[]{:S(2)}) async-start(), calls=%async_computation.11 | async-start | bytes 3538944 | tf_op jit(solution)/shard_map/all_gather | solution.py:941
  32.0 12.2 %collective-permute-start = (bf16[128,2048]{1,0:T(8,128)(2,1)S(1)}, bf16[128,2048]{1,0:T(8,128)(2,1)S(1)}, u32[]{:S(2)}, u32[]{:S(2)}) collective-permute-start(bf16[128,2048]{1,0:T(8,128)(2,1)S(1)} %get-tuple-element.318), channel_id=1, source_target_pairs={{0,8},{8,0},{16,24},{24,16},{1,9},{9,1},{17,25},{25,17},{2,10},{10... | collective-permute-start | bytes 1572872 | tf_op jit(solution)/shard_map/ppermute | solution.py:809
  33.0 13.0 %collective-permute-start.1 = (bf16[128,2048]{1,0:T(8,128)(2,1)S(1)}, bf16[128,2048]{1,0:T(8,128)(2,1)S(1)}, u32[]{:S(2)}, u32[]{:S(2)}) collective-permute-start(bf16[128,2048]{1,0:T(8,128)(2,1)S(1)} %get-tuple-element.316), channel_id=1, source_target_pairs={{0,16},{8,24},{16,0},{24,8},{1,17},{9,25},{17,1},{25,9},{2,18},{10... | collective-permute-start | bytes 1572872 | tf_op jit(solution)/shard_map/ppermute | solution.py:809
  44.3 23.3 %collective-permute-start.2 = (bf16[256,2048]{1,0:T(8,128)(2,1)S(1)}, bf16[256,2048]{1,0:T(8,128)(2,1)S(1)}, u32[]{:S(2)}, u32[]{:S(2)}) collective-permute-start(bf16[256,2048]{1,0:T(8,128)(2,1)S(1)} %pad_maximum_fusion.15), channel_id=1, source_target_pairs={{0,16},{8,24},{16,0},{24,8},{1,17},{9,25},{17,1},{25,9},{2,18},{10... | collective-permute-start | bytes 3145736 | tf_op jit(solution)/shard_map/ppermute | solution.py:809
  46.1 22.2 %collective-permute-start.3 = (bf16[256,2048]{1,0:T(8,128)(2,1)S(1)}, bf16[256,2048]{1,0:T(8,128)(2,1)S(1)}, u32[]{:S(2)}, u32[]{:S(2)}) collective-permute-start(bf16[256,2048]{1,0:T(8,128)(2,1)S(1)} %pad_maximum_fusion.16), channel_id=1, source_target_pairs={{0,8},{8,0},{16,24},{24,16},{1,9},{9,1},{17,25},{25,17},{2,10},{10... | collective-permute-start | bytes 3145736 | tf_op jit(solution)/shard_map/ppermute | solution.py:809
  90.8 93.2 %all-gather.15.cloned.1.call-start = ((), (), s32[]{:S(2)}) async-start(), calls=%async_computation.19 | async-start | bytes 4718592 | tf_op jit(solution)/shard_map/all_gather | solution.py:1093
  91.8 194.8 %all-gather.11.cloned.1.call-start = ((), (), s32[]{:S(2)}) async-start(), calls=%async_computation.12 | async-start | bytes 9437184 | tf_op jit(solution)/shard_map/all_gather | solution.py:941
  101.2 218.7 %all-gather.13.cloned.1.call-start = ((), (), s32[]{:S(2)}) async-start(), calls=%async_computation.13 | async-start | bytes 4718592 | tf_op jit(solution)/shard_map/all_gather | solution.py:1116
  114.9 12.5 %collective-permute-start.4 = (bf16[1024,128]{1,0:T(8,128)(2,1)}, bf16[1024,128]{1,0:T(8,128)(2,1)}, u32[]{:S(2)}, u32[]{:S(2)}) collective-permute-start(bf16[1024,128]{1,0:T(8,128)(2,1)} %get-tuple-element.291), channel_id=1, source_target_pairs={{0,8},{8,0},{16,24},{24,16},{1,9},{9,1},{17,25},{25,17},{2,10},{10... | collective-permute-start | bytes 786440 | tf_op jit(solution)/shard_map/ppermute | solution.py:809
  115.6 11.8 %collective-permute-start.5 = (bf16[1024,128]{1,0:T(8,128)(2,1)}, bf16[1024,128]{1,0:T(8,128)(2,1)}, u32[]{:S(2)}, u32[]{:S(2)}) collective-permute-start(bf16[1024,128]{1,0:T(8,128)(2,1)} %get-tuple-element.291), channel_id=1, source_target_pairs={{0,16},{8,24},{16,0},{24,8},{1,17},{9,25},{17,1},{25,9},{2,18},{10... | collective-permute-start | bytes 786440 | tf_op jit(solution)/shard_map/ppermute | solution.py:809
  116.1 14.1 %collective-permute-start.6 = (bf16[1024,128]{1,0:T(8,128)(2,1)}, bf16[1024,128]{1,0:T(8,128)(2,1)}, u32[]{:S(2)}, u32[]{:S(2)}) collective-permute-start(bf16[1024,128]{1,0:T(8,128)(2,1)} %get-tuple-element.291), channel_id=1, source_target_pairs={{0,24},{8,16},{16,8},{24,0},{1,25},{9,17},{17,9},{25,1},{2,26},{10... | collective-permute-start | bytes 786440 | tf_op jit(solution)/shard_map/ppermute | solution.py:809
  119.3 17.2 %collective-permute-start.8 = (bf16[128,2048]{1,0:T(8,128)(2,1)}, bf16[128,2048]{1,0:T(8,128)(2,1)}, u32[]{:S(2)}, u32[]{:S(2)}) collective-permute-start(bf16[128,2048]{1,0:T(8,128)(2,1)} %get-tuple-element.314), channel_id=1, source_target_pairs={{0,16},{8,24},{16,0},{24,8},{1,17},{9,25},{17,1},{25,9},{2,18},{10... | collective-permute-start | bytes 1572872 | tf_op jit(solution)/shard_map/ppermute | solution.py:809
  120.0 17.8 %collective-permute-start.7 = (bf16[128,2048]{1,0:T(8,128)(2,1)S(1)}, bf16[128,2048]{1,0:T(8,128)(2,1)}, u32[]{:S(2)}, u32[]{:S(2)}) collective-permute-start(bf16[128,2048]{1,0:T(8,128)(2,1)S(1)} %get-tuple-element.315), channel_id=1, source_target_pairs={{0,8},{8,0},{16,24},{24,16},{1,9},{9,1},{17,25},{25,17},{2,10},{10... | collective-permute-start | bytes 1572872 | tf_op jit(solution)/shard_map/ppermute | solution.py:809
  138.9 22.4 %collective-permute-start.10 = (bf16[256,2048]{1,0:T(8,128)(2,1)S(1)}, bf16[256,2048]{1,0:T(8,128)(2,1)S(1)}, u32[]{:S(2)}, u32[]{:S(2)}) collective-permute-start(bf16[256,2048]{1,0:T(8,128)(2,1)S(1)} %pad_maximum_fusion.19), channel_id=1, source_target_pairs={{0,8},{8,0},{16,24},{24,16},{1,9},{9,1},{17,25},{25,17},{2,10},{10... | collective-permute-start | bytes 3145736 | tf_op jit(solution)/shard_map/ppermute | solution.py:809
  139.8 21.5 %collective-permute-start.9 = (bf16[256,2048]{1,0:T(8,128)(2,1)S(1)}, bf16[256,2048]{1,0:T(8,128)(2,1)S(1)}, u32[]{:S(2)}, u32[]{:S(2)}) collective-permute-start(bf16[256,2048]{1,0:T(8,128)(2,1)S(1)} %pad_maximum_fusion.18), channel_id=1, source_target_pairs={{0,16},{8,24},{16,0},{24,8},{1,17},{9,25},{17,1},{25,9},{2,18},{10... | collective-permute-start | bytes 3145736 | tf_op jit(solution)/shard_map/ppermute | solution.py:809
  191.1 25.1 %collective-permute-start.14 = (bf16[256,2048]{1,0:T(8,128)(2,1)S(1)}, bf16[256,2048]{1,0:T(8,128)(2,1)S(1)}, u32[]{:S(2)}, u32[]{:S(2)}) collective-permute-start(bf16[256,2048]{1,0:T(8,128)(2,1)S(1)} %get-tuple-element.298), channel_id=1, source_target_pairs={{0,16},{8,24},{16,0},{24,8},{1,17},{9,25},{17,1},{25,9},{2,18},{10... | collective-permute-start | bytes 3145736 | tf_op jit(solution)/shard_map/ppermute | solution.py:809
  192.4 25.0 %collective-permute-start.16 = (bf16[256,2048]{1,0:T(8,128)(2,1)S(1)}, bf16[256,2048]{1,0:T(8,128)(2,1)S(1)}, u32[]{:S(2)}, u32[]{:S(2)}) collective-permute-start(bf16[256,2048]{1,0:T(8,128)(2,1)S(1)} %get-tuple-element.299), channel_id=1, source_target_pairs={{0,8},{8,0},{16,24},{24,16},{1,9},{9,1},{17,25},{25,17},{2,10},{10... | collective-permute-start | bytes 3145736 | tf_op jit(solution)/shard_map/ppermute | solution.py:809
  218.4 13.1 %collective-permute-start.15 = (bf16[128,2048]{1,0:T(8,128)(2,1)S(1)}, bf16[128,2048]{1,0:T(8,128)(2,1)S(1)}, u32[]{:S(2)}, u32[]{:S(2)}) collective-permute-start(bf16[128,2048]{1,0:T(8,128)(2,1)S(1)} %slice.1521), channel_id=1, source_target_pairs={{0,8},{8,0},{16,24},{24,16},{1,9},{9,1},{17,25},{25,17},{2,10},{10... | collective-permute-start | bytes 1572872 | tf_op jit(solution)/shard_map/ppermute | solution.py:809
  220.0 12.8 %collective-permute-start.17 = (bf16[128,2048]{1,0:T(8,128)(2,1)S(1)}, bf16[128,2048]{1,0:T(8,128)(2,1)S(1)}, u32[]{:S(2)}, u32[]{:S(2)}) collective-permute-start(bf16[128,2048]{1,0:T(8,128)(2,1)S(1)} %slice.1520), channel_id=1, source_target_pairs={{0,16},{8,24},{16,0},{24,8},{1,17},{9,25},{17,1},{25,9},{2,18},{10... | collective-permute-start | bytes 1572872 | tf_op jit(solution)/shard_map/ppermute | solution.py:809
  235.3 12.3 %collective-permute-start.18 = (bf16[128,2048]{1,0:T(8,128)(2,1)}, bf16[128,2048]{1,0:T(8,128)(2,1)}, u32[]{:S(2)}, u32[]{:S(2)}) collective-permute-start(bf16[128,2048]{1,0:T(8,128)(2,1)} %get-tuple-element.310), channel_id=1, source_target_pairs={{0,8},{8,0},{16,24},{24,16},{1,9},{9,1},{17,25},{25,17},{2,10},{10... | collective-permute-start | bytes 1572872 | tf_op jit(solution)/shard_map/ppermute | solution.py:809
  235.9 154.2 %reduce-scatter.6.cloned.1.call-start = ((), (), s32[]{:S(2)}) async-start(), calls=%async_computation.14 | async-start | bytes 4718592 | tf_op jit(solution)/shard_map/reduce_scatter | solution.py:1171
  251.5 14.9 %collective-permute-start.20 = (bf16[128,2048]{1,0:T(8,128)(2,1)S(1)}, bf16[128,2048]{1,0:T(8,128)(2,1)S(1)}, u32[]{:S(2)}, u32[]{:S(2)}) collective-permute-start(bf16[128,2048]{1,0:T(8,128)(2,1)S(1)} %get-tuple-element.308), channel_id=1, source_target_pairs={{0,16},{8,24},{16,0},{24,8},{1,17},{9,25},{17,1},{25,9},{2,18},{10... | collective-permute-start | bytes 1572872 | tf_op jit(solution)/shard_map/ppermute | solution.py:809
  253.5 31.5 %collective-permute-start.19 = (bf16[256,2048]{1,0:T(8,128)(2,1)S(1)}, bf16[256,2048]{1,0:T(8,128)(2,1)S(1)}, u32[]{:S(2)}, u32[]{:S(2)}) collective-permute-start(bf16[256,2048]{1,0:T(8,128)(2,1)S(1)} %pad_maximum_fusion.20), channel_id=1, source_target_pairs={{0,16},{8,24},{16,0},{24,8},{1,17},{9,25},{17,1},{25,9},{2,18},{10... | collective-permute-start | bytes 3145736 | tf_op jit(solution)/shard_map/ppermute | solution.py:809
  266.5 18.5 %collective-permute-start.21 = (bf16[256,2048]{1,0:T(8,128)(2,1)S(1)}, bf16[256,2048]{1,0:T(8,128)(2,1)S(1)}, u32[]{:S(2)}, u32[]{:S(2)}) collective-permute-start(bf16[256,2048]{1,0:T(8,128)(2,1)S(1)} %pad_maximum_fusion.21), channel_id=1, source_target_pairs={{0,8},{8,0},{16,24},{24,16},{1,9},{9,1},{17,25},{25,17},{2,10},{10... | collective-permute-start | bytes 3145736 | tf_op jit(solution)/shard_map/ppermute | solution.py:809
  314.8 159.3 %reduce-scatter.8.cloned.1.call-start = ((), (), s32[]{:S(2)}) async-start(), calls=%async_computation.15 | async-start | bytes 9437184 | tf_op jit(solution)/shard_map/reduce_scatter | solution.py:1182
  352.0 197.7 %reduce-scatter.10.cloned.1.call-start = ((), (), s32[]{:S(2)}) async-start(), calls=%async_computation.16 | async-start | bytes 4718592 | tf_op jit(solution)/shard_map/reduce_scatter | solution.py:1212
  354.0 21.3 %collective-permute-start.22 = (bf16[256,2048]{1,0:T(8,128)(2,1)S(1)}, bf16[256,2048]{1,0:T(8,128)(2,1)S(1)}, u32[]{:S(2)}, u32[]{:S(2)}) collective-permute-start(bf16[256,2048]{1,0:T(8,128)(2,1)S(1)} %get-tuple-element.296), channel_id=1, source_target_pairs={{0,16},{8,24},{16,0},{24,8},{1,17},{9,25},{17,1},{25,9},{2,18},{10... | collective-permute-start | bytes 3145736 | tf_op jit(solution)/shard_map/ppermute | solution.py:809
  354.9 22.3 %collective-permute-start.24 = (bf16[256,2048]{1,0:T(8,128)(2,1)S(1)}, bf16[256,2048]{1,0:T(8,128)(2,1)S(1)}, u32[]{:S(2)}, u32[]{:S(2)}) collective-permute-start(bf16[256,2048]{1,0:T(8,128)(2,1)S(1)} %get-tuple-element.297), channel_id=1, source_target_pairs={{0,8},{8,0},{16,24},{24,16},{1,9},{9,1},{17,25},{25,17},{2,10},{10... | collective-permute-start | bytes 3145736 | tf_op jit(solution)/shard_map/ppermute | solution.py:809
  394.9 12.8 %collective-permute-start.26 = (bf16[128,2048]{1,0:T(8,128)(2,1)S(1)}, bf16[128,2048]{1,0:T(8,128)(2,1)S(1)}, u32[]{:S(2)}, u32[]{:S(2)}) collective-permute-start(bf16[128,2048]{1,0:T(8,128)(2,1)S(1)} %get-tuple-element.313), channel_id=1, source_target_pairs={{0,8},{8,0},{16,24},{24,16},{1,9},{9,1},{17,25},{25,17},{2,10},{10... | collective-permute-start | bytes 1572872 | tf_op jit(solution)/shard_map/ppermute | solution.py:809
  396.1 14.8 %collective-permute-start.27 = (bf16[128,2048]{1,0:T(8,128)(2,1)S(1)}, bf16[128,2048]{1,0:T(8,128)(2,1)S(1)}, u32[]{:S(2)}, u32[]{:S(2)}) collective-permute-start(bf16[128,2048]{1,0:T(8,128)(2,1)S(1)} %get-tuple-element.311), channel_id=1, source_target_pairs={{0,16},{8,24},{16,0},{24,8},{1,17},{9,25},{17,1},{25,9},{2,18},{10... | collective-permute-start | bytes 1572872 | tf_op jit(solution)/shard_map/ppermute | solution.py:809
  407.8 19.7 %collective-permute-start.28 = (bf16[256,2048]{1,0:T(8,128)(2,1)S(1)}, bf16[256,2048]{1,0:T(8,128)(2,1)S(1)}, u32[]{:S(2)}, u32[]{:S(2)}) collective-permute-start(bf16[256,2048]{1,0:T(8,128)(2,1)S(1)} %pad_maximum_fusion.22), channel_id=1, source_target_pairs={{0,16},{8,24},{16,0},{24,8},{1,17},{9,25},{17,1},{25,9},{2,18},{10... | collective-permute-start | bytes 3145736 | tf_op jit(solution)/shard_map/ppermute | solution.py:809
  411.0 16.5 %collective-permute-start.29 = (bf16[256,2048]{1,0:T(8,128)(2,1)S(1)}, bf16[256,2048]{1,0:T(8,128)(2,1)S(1)}, u32[]{:S(2)}, u32[]{:S(2)}) collective-permute-start(bf16[256,2048]{1,0:T(8,128)(2,1)S(1)} %pad_maximum_fusion.23), channel_id=1, source_target_pairs={{0,8},{8,0},{16,24},{24,16},{1,9},{9,1},{17,25},{25,17},{2,10},{10... | collective-permute-start | bytes 3145736 | tf_op jit(solution)/shard_map/ppermute | solution.py:809
  436.0 11.3 %collective-permute-start.30 = (f32[1024]{0:T(1024)S(1)}, f32[1024]{0:T(1024)S(1)}, u32[]{:S(2)}, u32[]{:S(2)}) collective-permute-start(f32[1024]{0:T(1024)S(1)} %get-tuple-element.461), channel_id=1, source_target_pairs={{0,8},{8,0},{16,24},{24,16},{1,9},{9,1},{17,25},{25,17},{2,10},{10... | collective-permute-start | bytes 12296 | tf_op jit(solution)/shard_map/ppermute | solution.py:809
  447.5 133.4 %reduce-scatter.12.cloned.1.call-start = ((), (), s32[]{:S(2)}) async-start(), calls=%async_computation.17 | async-start | bytes 5898240 | tf_op jit(solution)/shard_map/reduce_scatter | solution.py:1224
  477.2 44.5 %collective-permute-start.33 = (bf16[256,2048]{1,0:T(8,128)(2,1)}, bf16[256,2048]{1,0:T(8,128)(2,1)}, u32[]{:S(2)}, u32[]{:S(2)}) collective-permute-start(bf16[256,2048]{1,0:T(8,128)(2,1)} %get-tuple-element.295), channel_id=1, source_target_pairs={{0,16},{8,24},{16,0},{24,8},{1,17},{9,25},{17,1},{25,9},{2,18},{10... | collective-permute-start | bytes 3145736 | tf_op jit(solution)/shard_map/ppermute | solution.py:809
  478.5 43.3 %collective-permute-start.34 = (bf16[256,2048]{1,0:T(8,128)(2,1)}, bf16[256,2048]{1,0:T(8,128)(2,1)}, u32[]{:S(2)}, u32[]{:S(2)}) collective-permute-start(bf16[256,2048]{1,0:T(8,128)(2,1)} %get-tuple-element.294), channel_id=1, source_target_pairs={{0,8},{8,0},{16,24},{24,16},{1,9},{9,1},{17,25},{25,17},{2,10},{10... | collective-permute-start | bytes 3145736 | tf_op jit(solution)/shard_map/ppermute | solution.py:809
  522.7 14.4 %collective-permute-start.35 = (bf16[1024,128]{1,0:T(8,128)(2,1)}, bf16[1024,128]{1,0:T(8,128)(2,1)S(1)}, u32[]{:S(2)}, u32[]{:S(2)}) collective-permute-start(bf16[1024,128]{1,0:T(8,128)(2,1)} %get-tuple-element.304), channel_id=1, source_target_pairs={{0,8},{8,0},{16,24},{24,16},{1,9},{9,1},{17,25},{25,17},{2,10},{10... | collective-permute-start | bytes 786440 | tf_op jit(solution)/shard_map/ppermute | solution.py:809
  523.7 13.4 %collective-permute-start.36 = (bf16[1024,128]{1,0:T(8,128)(2,1)}, bf16[1024,128]{1,0:T(8,128)(2,1)S(1)}, u32[]{:S(2)}, u32[]{:S(2)}) collective-permute-start(bf16[1024,128]{1,0:T(8,128)(2,1)} %get-tuple-element.306), channel_id=1, source_target_pairs={{0,16},{8,24},{16,0},{24,8},{1,17},{9,25},{17,1},{25,9},{2,18},{10... | collective-permute-start | bytes 786440 | tf_op jit(solution)/shard_map/ppermute | solution.py:809
  524.5 12.6 %collective-permute-start.37 = (bf16[1024,128]{1,0:T(8,128)(2,1)}, bf16[1024,128]{1,0:T(8,128)(2,1)S(1)}, u32[]{:S(2)}, u32[]{:S(2)}) collective-permute-start(bf16[1024,128]{1,0:T(8,128)(2,1)} %get-tuple-element.305), channel_id=1, source_target_pairs={{0,24},{8,16},{16,8},{24,0},{1,25},{9,17},{17,9},{25,1},{2,26},{10... | collective-permute-start | bytes 786440 | tf_op jit(solution)/shard_map/ppermute | solution.py:809
  532.5 17.5 %all-to-all-start.2 = ((bf16[4,64,2048]{2,1,0:T(8,128)(2,1)}), bf16[4,64,2048]{2,1,0:T(8,128)(2,1)}, u32[]{:S(2)}, u32[]{:S(2)}) async-start(bf16[4,64,2048]{2,1,0:T(8,128)(2,1)} %reduce-scatter.8.cloned.1.call-done), calls=%async_computation.5 | async-start | bytes 2097152 | tf_op jit(solution)/shard_map/all_to_all | solution.py:950
  536.8 86.2 %reduce-scatter.14.cloned.1.call-start = ((), (), s32[]{:S(2)}) async-start(), calls=%async_computation.18 | async-start | bytes 4718592 | tf_op jit(solution)/shard_map/reduce_scatter | solution.py:1272
  544.7 15.6 %collective-permute-start.38 = (bf16[128,2048]{1,0:T(8,128)(2,1)}, bf16[128,2048]{1,0:T(8,128)(2,1)S(1)}, u32[]{:S(2)}, u32[]{:S(2)}) collective-permute-start(bf16[128,2048]{1,0:T(8,128)(2,1)} %slice.1517), channel_id=1, source_target_pairs={{0,8},{8,0},{16,24},{24,16},{1,9},{9,1},{17,25},{25,17},{2,10},{10... | collective-permute-start | bytes 1572872 | tf_op jit(solution)/shard_map/ppermute | solution.py:809
  546.6 13.6 %collective-permute-start.39 = (bf16[128,2048]{1,0:T(8,128)(2,1)}, bf16[128,2048]{1,0:T(8,128)(2,1)}, u32[]{:S(2)}, u32[]{:S(2)}) collective-permute-start(bf16[128,2048]{1,0:T(8,128)(2,1)} %slice.1516), channel_id=1, source_target_pairs={{0,16},{8,24},{16,0},{24,8},{1,17},{9,25},{17,1},{25,9},{2,18},{10... | collective-permute-start | bytes 1572872 | tf_op jit(solution)/shard_map/ppermute | solution.py:809
  567.5 25.1 %collective-permute-start.40 = (bf16[256,2048]{1,0:T(8,128)(2,1)}, bf16[256,2048]{1,0:T(8,128)(2,1)}, u32[]{:S(2)}, u32[]{:S(2)}) collective-permute-start(bf16[256,2048]{1,0:T(8,128)(2,1)} %get-tuple-element.293), channel_id=1, source_target_pairs={{0,16},{8,24},{16,0},{24,8},{1,17},{9,25},{17,1},{25,9},{2,18},{10... | collective-permute-start | bytes 3145736 | tf_op jit(solution)/shard_map/ppermute | solution.py:809
  569.1 23.4 %collective-permute-start.41 = (bf16[256,2048]{1,0:T(8,128)(2,1)}, bf16[256,2048]{1,0:T(8,128)(2,1)}, u32[]{:S(2)}, u32[]{:S(2)}) collective-permute-start(bf16[256,2048]{1,0:T(8,128)(2,1)} %get-tuple-element.292), channel_id=1, source_target_pairs={{0,8},{8,0},{16,24},{24,16},{1,9},{9,1},{17,25},{25,17},{2,10},{10... | collective-permute-start | bytes 3145736 | tf_op jit(solution)/shard_map/ppermute | solution.py:809
  580.9 11.6 %all-to-all-start.3 = ((bf16[4,64,1280]{2,1,0:T(8,128)(2,1)}), bf16[4,64,1280]{2,1,0:T(8,128)(2,1)S(1)}, u32[]{:S(2)}, u32[]{:S(2)}) async-start(bf16[4,64,1280]{2,1,0:T(8,128)(2,1)} %reduce-scatter.12.cloned.1.call-done), calls=%async_computation.7 | async-start | bytes 1310720 | tf_op jit(solution)/shard_map/all_to_all | solution.py:950
  596.6 13.4 %collective-permute-start.42 = (bf16[128,2048]{1,0:T(8,128)(2,1)S(1)}, bf16[128,2048]{1,0:T(8,128)(2,1)S(1)}, u32[]{:S(2)}, u32[]{:S(2)}) collective-permute-start(bf16[128,2048]{1,0:T(8,128)(2,1)S(1)} %slice.1515), channel_id=1, source_target_pairs={{0,8},{8,0},{16,24},{24,16},{1,9},{9,1},{17,25},{25,17},{2,10},{10... | collective-permute-start | bytes 1572872 | tf_op jit(solution)/shard_map/ppermute | solution.py:809
  (128 other events, 1626.0 us)
Sparse Core Ops, SparseCore 0:
  31.9 64.4 all-gather.6
  98.5 36.9 all-gather.8
  137.7 45.9 all-gather.14
  185.8 80.7 all-gather.10
  268.1 45.7 all-gather.12
  316.0 48.7 reduce-scatter.5
  367.0 87.7 reduce-scatter.7
  457.1 48.3 reduce-scatter.9
  507.8 58.0 reduce-scatter.11
  575.1 47.9 reduce-scatter.13
